TPU v7x, 128 devices: a whole 4x4x4 slice. The times are simulated.
128 devices in a mesh: gx: 8 (over x, core), gy: 4 (over y), gz: 4 (over z).
Axes of the slice: x: 4, y: 4, z: 4, core: 2. Of those that a mesh axis runs over, the one named last changes fastest.
Arguments:
- rhs: float32 [8, 4, 4, 1024, 128], P('gx', 'gy', 'gz'), may hold values from -40 to 40
- diagonal: float32 [8, 4, 4, 1024], P('gx', 'gy', 'gz'), may hold values from 0.05 to 1
- couple: float32 [8, 4, 4, 6, 1024], P('gx', 'gy', 'gz'), may hold values from 0 to 1
- neighbours: int32 [8, 4, 4, 6, 1024], P('gx', 'gy', 'gz'), may hold values from 0 to 2559
- export_rows: int32 [8, 4, 4, 6, 256], P('gx', 'gy', 'gz'), may hold values from 0 to 1023
- local_inverse: float32 [8, 4, 4, 1024, 2560], P('gx', 'gy', 'gz'), may hold values from -1 to 1
- basis: float32 [8, 4, 4, 64, 1024], P('gx', 'gy', 'gz'), may hold values from -0.1875 to 0.1875
- coarse_inverse: float32 [8192, 8192], P(('gx', 'gy', 'gz')), may hold values from -1 to 1
- owner: int32 [128], replicated, may hold values from 0 to 127, each once
Outputs:
- solution: float32 [8, 4, 4, 1024, 128], P('gx', 'gy', 'gz')
- residual: float32 [8, 4, 4, 1024, 128], P('gx', 'gy', 'gz')
Inputs may be any that keep to these rules, and one draw needn't show every extreme that they name: `owner`: each coarse block belongs to exactly one subdomain.
All inputs are finite; a program needn't handle non-finite values.
Results may differ from a plain program's by a relative error of at most 0.0001.
Values sent between devices are 32-bit elements; how exact they have to be, the bound alone decides.
A program may use at most 128 MiB of HBM per device.

v0:
```python
import jax
import jax.numpy as jnp
from jax import lax
from jax.sharding import PartitionSpec as P

ITERS = 2


def with_halo(x, sides, width):
    for axis, dim in sides:
        peers, length = (lax.axis_size(axis), x.shape[dim])
        up = [(i, (i + 1) % peers) for i in range(peers - 1)]
        down = [(j, i) for i, j in up]
        last = lax.slice_in_dim(x, length - width, length, axis=dim)
        initial = lax.slice_in_dim(x, 0, width, axis=dim)
        before = lax.ppermute(last, axis, up)
        after = lax.ppermute(initial, axis, down)
        x = jnp.concatenate([before, x, after], axis=dim)
    return x


def product(left, right):
    return jnp.dot(left, right, precision=lax.Precision.HIGHEST)


def extend(field, exports):
    outgoing = field[exports]
    along_x = with_halo(outgoing[0:2], (("gx", 0),), 1)
    along_y = with_halo(outgoing[2:4], (("gy", 0),), 1)
    along_z = with_halo(outgoing[4:6], (("gz", 0),), 1)
    pieces = [along_x[0], along_x[3], along_y[0], along_y[3], along_z[0], along_z[3]]
    return jnp.concatenate([field] + pieces, axis=0)


def operate(field, diag_rows, couple_rows, links, exports):
    whole = extend(field, exports)
    picked = whole[links]
    return (6.0 + diag_rows)[:, None] * field - jnp.sum(couple_rows[:, :, None] * picked, axis=0)


def step_totals(cross_part, energy_part):
    return lax.psum((cross_part, energy_part), ("gx", "gy", "gz"))


def body(
    rhs, diagonal, couple, neighbours, export_rows, local_inverse, basis, coarse_inverse, owner
):
    field = rhs.reshape(rhs.shape[3:])
    diag_rows = diagonal.reshape(diagonal.shape[3:])
    couple_rows = couple.reshape(couple.shape[3:])
    links = neighbours.reshape(neighbours.shape[3:])
    exports = export_rows.reshape(export_rows.shape[3:])
    inverse_block = local_inverse.reshape(local_inverse.shape[3:])
    vectors = basis.reshape(basis.shape[3:])
    members = lax.axis_size(("gx", "gy", "gz"))
    position = lax.axis_index(("gx", "gy", "gz"))
    target = owner[position]
    source_order = jnp.argsort(owner)
    columns = field.shape[1]
    solution = jnp.zeros_like(field)
    residual = field
    coarse = jnp.zeros((members, vectors.shape[0], columns), jnp.float32)
    for sweep in range(ITERS):
        local = product(inverse_block, extend(residual, exports))
        projected = product(vectors, residual)
        everyone = lax.all_gather(projected[None], ("gx", "gy", "gz"), axis=0, tiled=True)
        coarse = everyone[source_order]
        solved = product(coarse_inverse, coarse.reshape(-1, columns))
        gathered = lax.all_gather(solved[None], ("gx", "gy", "gz"), axis=0, tiled=True)
        mapped = lax.dynamic_index_in_dim(gathered, target, 0, keepdims=False)
        update = local + product(vectors.T, mapped)
        image = operate(update, diag_rows, couple_rows, links, exports)
        cross_part = jnp.sum(residual * image, axis=0)
        energy_part = jnp.sum(image * image, axis=0)
        cross, energy = step_totals(cross_part, energy_part)
        alpha = cross / energy
        solution = solution + alpha * update
        residual = residual - alpha * image
    return (solution.reshape(rhs.shape), residual.reshape(rhs.shape))


def solution(mesh):
    placed = (
        P("gx", "gy", "gz", None, None),
        P("gx", "gy", "gz", None),
        P("gx", "gy", "gz", None, None),
        P("gx", "gy", "gz", None, None),
        P("gx", "gy", "gz", None, None),
        P("gx", "gy", "gz", None, None),
        P("gx", "gy", "gz", None, None),
        P(("gx", "gy", "gz"), None),
        P(),
    )
    return jax.shard_map(
        body,
        mesh=mesh,
        in_specs=placed,
        out_specs=(P("gx", "gy", "gz", None, None), P("gx", "gy", "gz", None, None)),
        check_vma=False,
    )
```

profile of v0, /device:TPU:1, one launch (start us, length us, event | category | flops | bytes accessed | tf_op | source)
XLA Modules:
  0.0 575.6 jit_solution(1505944343521835163)
XLA Ops:
  7.2 2.3 fusion.22
  9.6 3.2 sort.17
  12.8 69.4 %all-gather.9.cloned.1.call-done = f32[8192,128]{1,0:T(8,128)} async-done(((f32[64,128]{1,0:T(8,128)}), f32[8192,128]{1,0:T(8,128)}) %all-gather.9.cloned.1.call-update) | async-done | bytes 4194320 | tf_op jit(solution)/shard_map/all_gather | solution.py:66
  82.2 5.0 gather_fusion.1
  87.2 5.1 convolution_bitcast_fusion.2
  92.5 2.6 gather_fusion
  101.3 3.0 collective-permute-start.1
  105.9 2.5 collective-permute-start.2
  129.9 27.0 %all-gather.11.cloned.1.call-done = f32[8192,128]{1,0:T(8,128)} async-done(((f32[64,128]{1,0:T(8,128)}), f32[8192,128]{1,0:T(8,128)}) %all-gather.11.cloned.1.call-update) | async-done | bytes 4194320 | tf_op jit(solution)/shard_map/all_gather | solution.py:69
  158.3 15.9 %constant_dynamic-update-slice_fusion = (f32[2560,128]{0,1:T(8,128)}, f32[1024,128]{0,1:T(8,128)S(1)}) fusion(f32[128,1024]{1,0:T(8,128)S(1)} %fusion.20, f32[2560,128]{0,1:T(8,128)} %bitcast_dynamic-update-slice_fusion.19, f32[1,1,1,1024,2560]{4,3,2,1,0:T(8,128)} %param.14), kind=kOutput, calls=%fused_computation.64 | convolution fusion | flops 4026662912 | bytes 13369344 | tf_op jit(solution)/shard_map/dot_general | solution.py:23
  174.3 3.7 gather_fusion.2
  181.9 2.3 collective-permute-start.7
  187.4 2.3 collective-permute-start.10
  199.2 20.9 %gather_fusion.3 = f32[6144,128]{1,0:T(8,128)} fusion(f32[2560,128]{1,0:T(8,128)S(1)} %copy.59, s32[6144]{0:T(1024)S(1)} %broadcast_clamp_fusion), kind=kCustom, calls=%fused_computation.3 | custom fusion | bytes 6316032 | tf_op jit(solution)/shard_map/gather | solution.py:37
  220.2 3.2 multiply_reduce_fusion.1
  227.5 65.3 %all-reduce.1 = (f32[128]{0:T(128)S(1)}, f32[128]{0:T(128)S(1)}) all-reduce(f32[128]{0:T(128)S(1)} %get-tuple-element.11, f32[128]{0:T(128)S(1)} %get-tuple-element.10), channel_id=1, replica_groups=mesh['gx'=8,'gy'=4,'gz'=4] {'gx','gy','gz'}, use_global_device_ids=true, to_apply=%region_3.4 | all-reduce | flops 256 | bytes 2048 | tf_op jit(solution)/shard_map/psum | solution.py:42
  296.3 64.6 %all-gather.13.cloned.1.call-done = f32[8192,128]{1,0:T(8,128)} async-done(((f32[64,128]{1,0:T(8,128)}), f32[8192,128]{1,0:T(8,128)}) %all-gather.13.cloned.1.call-update) | async-done | bytes 4194320 | tf_op jit(solution)/shard_map/all_gather | solution.py:66
  360.9 5.0 gather_fusion.5
  365.9 5.1 convolution_bitcast_fusion.1
  371.2 2.6 gather_fusion.4
  377.8 3.0 collective-permute-start.13
  383.9 2.3 collective-permute-start.16
  390.1 3.2 collective-permute-done.17
  393.4 42.1 %all-gather.15.cloned.1.call-done = f32[8192,128]{1,0:T(8,128)} async-done(((f32[64,128]{1,0:T(8,128)}), f32[8192,128]{1,0:T(8,128)}) %all-gather.15.cloned.1.call-update) | async-done | bytes 4194320 | tf_op jit(solution)/shard_map/all_gather | solution.py:69
  436.9 14.3 %constant_dynamic-update-slice_fusion.2 = (f32[2560,128]{0,1:T(8,128)}, f32[1024,128]{0,1:T(8,128)S(1)}) fusion(f32[128,1024]{1,0:T(8,128)S(1)} %fusion.17, f32[2560,128]{0,1:T(8,128)S(1)} %bitcast_dynamic-update-slice_fusion.7, f32[1,1,1,1024,2560]{4,3,2,1,0:T(8,128)} %param.14), kind=kOutput, calls=%fused_computation.66 | convolution fusion | flops 4026662912 | bytes 13369344 | tf_op jit(solution)/shard_map/dot_general | solution.py:23
  451.3 2.6 gather_fusion.6
  456.6 2.3 collective-permute-start.19
  462.1 2.3 collective-permute-start.22
  473.9 20.9 %gather_fusion.7 = f32[6144,128]{1,0:T(8,128)} fusion(f32[2560,128]{1,0:T(8,128)S(1)} %copy.75, s32[6144]{0:T(1024)S(1)} %broadcast_clamp_fusion), kind=kCustom, calls=%fused_computation.7 | custom fusion | bytes 6316032 | tf_op jit(solution)/shard_map/gather | solution.py:37
  494.9 2.4 multiply_reduce_fusion
  498.4 65.0 %all-reduce = (f32[128]{0:T(128)S(1)}, f32[128]{0:T(128)S(1)}) all-reduce(f32[128]{0:T(128)S(1)} %get-tuple-element.9, f32[128]{0:T(128)S(1)} %get-tuple-element.8), channel_id=1, replica_groups=mesh['gx'=8,'gy'=4,'gz'=4] {'gx','gy','gz'}, use_global_device_ids=true, to_apply=%region_8.9 | all-reduce | flops 256 | bytes 2048 | tf_op jit(solution)/shard_map/psum | solution.py:42
  563.4 2.5 subtract_bitcast_fusion
  (161 shorter events, 85.2 us)
Async XLA Ops:
  7.2 80.0 %copy-start = (f32[64,8192]{1,0:T(8,128)S(1)}, f32[64,8192]{1,0:T(8,128)}, u32[]{:S(2)}) copy-start(f32[64,8192]{1,0:T(8,128)} %param.16) | copy-start | bytes 6291460
  7.2 75.1 %all-gather.9.cloned.1.call-start = ((), (), s32[]{:S(2)}) async-start(), calls=%async_computation | async-start | bytes 4227072 | tf_op jit(solution)/shard_map/all_gather | solution.py:66
  9.6 147.3 %all-gather.11.cloned.1.call-start = ((), (), s32[]{:S(2)}) async-start(), calls=%async_computation.1 | async-start | bytes 4227072 | tf_op jit(solution)/shard_map/all_gather | solution.py:69
  92.4 268.5 %all-gather.13.cloned.1.call-start = ((), (), s32[]{:S(2)}) async-start(), calls=%async_computation.2 | async-start | bytes 4227072 | tf_op jit(solution)/shard_map/all_gather | solution.py:66
  97.6 23.1 %collective-permute-start = (f32[1,256,128]{1,2,0:T(8,128)}, f32[1,256,128]{1,2,0:T(8,128)}, u32[]{:S(2)}, u32[]{:S(2)}) collective-permute-start(f32[1,256,128]{1,2,0:T(8,128)} %bitcast.4), channel_id=1, source_target_pairs={{0,16},{16,32},{32,48},{48,64},{64,80},{80,96},{96,112},{1,17},{17... | collective-permute-start | bytes 393224 | tf_op jit(solution)/shard_map/ppermute | solution.py:16
  101.3 22.5 %collective-permute-start.1 = (f32[1,256,128]{1,2,0:T(8,128)}, f32[1,256,128]{1,2,0:T(8,128)}, u32[]{:S(2)}, u32[]{:S(2)}) collective-permute-start(f32[1,256,128]{1,2,0:T(8,128)} %bitcast.6), channel_id=1, source_target_pairs={{16,0},{32,16},{48,32},{64,48},{80,64},{96,80},{112,96},{17,1},{33... | collective-permute-start | bytes 393224 | tf_op jit(solution)/shard_map/ppermute | solution.py:17
  105.9 19.4 %collective-permute-start.2 = (f32[1,256,128]{1,2,0:T(8,128)}, f32[1,256,128]{1,2,0:T(8,128)}, u32[]{:S(2)}, u32[]{:S(2)}) collective-permute-start(f32[1,256,128]{1,2,0:T(8,128)} %bitcast.8), channel_id=1, source_target_pairs={{0,4},{4,8},{8,12},{1,5},{5,9},{9,13},{2,6},{6,10},{10,14},{3,7},{... | collective-permute-start | bytes 393224 | tf_op jit(solution)/shard_map/ppermute | solution.py:16
  110.0 16.9 %collective-permute-start.3 = (f32[1,256,128]{1,2,0:T(8,128)}, f32[1,256,128]{1,2,0:T(8,128)}, u32[]{:S(2)}, u32[]{:S(2)}) collective-permute-start(f32[1,256,128]{1,2,0:T(8,128)} %bitcast.10), channel_id=1, source_target_pairs={{4,0},{8,4},{12,8},{5,1},{9,5},{13,9},{6,2},{10,6},{14,10},{7,3},{... | collective-permute-start | bytes 393224 | tf_op jit(solution)/shard_map/ppermute | solution.py:17
  112.3 16.1 %collective-permute-start.4 = (f32[1,256,128]{1,2,0:T(8,128)S(1)}, f32[1,256,128]{1,2,0:T(8,128)S(1)}, u32[]{:S(2)}, u32[]{:S(2)}) collective-permute-start(f32[1,256,128]{1,2,0:T(8,128)S(1)} %bitcast.163), channel_id=1, source_target_pairs={{0,1},{1,2},{2,3},{4,5},{5,6},{6,7},{8,9},{9,10},{10,11},{12,13},{... | collective-permute-start | bytes 393224 | tf_op jit(solution)/shard_map/ppermute | solution.py:16
  119.8 37.1 %copy-start.8 = (f32[1,1,1,64,1024]{4,3,2,1,0:T(8,128)S(1)}, f32[1,1,1,64,1024]{4,3,2,1,0:T(8,128)}, u32[]{:S(2)}) copy-start(f32[1,1,1,64,1024]{4,3,2,1,0:T(8,128)} %param.15) | copy-start | bytes 786436
  120.7 8.5 %collective-permute-start.5 = (f32[1,256,128]{1,2,0:T(8,128)S(1)}, f32[1,256,128]{1,2,0:T(8,128)S(1)}, u32[]{:S(2)}, u32[]{:S(2)}) collective-permute-start(f32[1,256,128]{1,2,0:T(8,128)S(1)} %bitcast.170), channel_id=1, source_target_pairs={{1,0},{2,1},{3,2},{5,4},{6,5},{7,6},{9,8},{10,9},{11,10},{13,12},{... | collective-permute-start | bytes 393224 | tf_op jit(solution)/shard_map/ppermute | solution.py:17
  179.4 10.3 %collective-permute-start.6 = (f32[1,256,128]{1,2,0:T(8,128)S(1)}, f32[1,256,128]{1,2,0:T(8,128)S(1)}, u32[]{:S(2)}, u32[]{:S(2)}) collective-permute-start(f32[1,256,128]{1,2,0:T(8,128)S(1)} %bitcast.177), channel_id=1, source_target_pairs={{0,16},{16,32},{32,48},{48,64},{64,80},{80,96},{96,112},{1,17},{17... | collective-permute-start | bytes 393224 | tf_op jit(solution)/shard_map/ppermute | solution.py:16
  181.9 9.8 %collective-permute-start.7 = (f32[1,256,128]{1,2,0:T(8,128)S(1)}, f32[1,256,128]{1,2,0:T(8,128)S(1)}, u32[]{:S(2)}, u32[]{:S(2)}) collective-permute-start(f32[1,256,128]{1,2,0:T(8,128)S(1)} %bitcast.180), channel_id=1, source_target_pairs={{16,0},{32,16},{48,32},{64,48},{80,64},{96,80},{112,96},{17,1},{33... | collective-permute-start | bytes 393224 | tf_op jit(solution)/shard_map/ppermute | solution.py:17
  184.3 8.1 %collective-permute-start.8 = (f32[1,256,128]{1,2,0:T(8,128)S(1)}, f32[1,256,128]{1,2,0:T(8,128)S(1)}, u32[]{:S(2)}, u32[]{:S(2)}) collective-permute-start(f32[1,256,128]{1,2,0:T(8,128)S(1)} %bitcast.174), channel_id=1, source_target_pairs={{0,4},{4,8},{8,12},{1,5},{5,9},{9,13},{2,6},{6,10},{10,14},{3,7},{... | collective-permute-start | bytes 393224 | tf_op jit(solution)/shard_map/ppermute | solution.py:16
  186.1 7.3 %collective-permute-start.9 = (f32[1,256,128]{1,2,0:T(8,128)S(1)}, f32[1,256,128]{1,2,0:T(8,128)S(1)}, u32[]{:S(2)}, u32[]{:S(2)}) collective-permute-start(f32[1,256,128]{1,2,0:T(8,128)S(1)} %bitcast.171), channel_id=1, source_target_pairs={{4,0},{8,4},{12,8},{5,1},{9,5},{13,9},{6,2},{10,6},{14,10},{7,3},{... | collective-permute-start | bytes 393224 | tf_op jit(solution)/shard_map/ppermute | solution.py:17
  187.4 6.7 %collective-permute-start.10 = (f32[1,256,128]{1,2,0:T(8,128)S(1)}, f32[1,256,128]{1,2,0:T(8,128)S(1)}, u32[]{:S(2)}, u32[]{:S(2)}) collective-permute-start(f32[1,256,128]{1,2,0:T(8,128)S(1)} %bitcast.167), channel_id=1, source_target_pairs={{0,1},{1,2},{2,3},{4,5},{5,6},{6,7},{8,9},{9,10},{10,11},{12,13},{... | collective-permute-start | bytes 393224 | tf_op jit(solution)/shard_map/ppermute | solution.py:16
  189.7 7.1 %collective-permute-start.11 = (f32[1,256,128]{1,2,0:T(8,128)S(1)}, f32[1,256,128]{1,2,0:T(8,128)S(1)}, u32[]{:S(2)}, u32[]{:S(2)}) collective-permute-start(f32[1,256,128]{1,2,0:T(8,128)S(1)} %bitcast.164), channel_id=1, source_target_pairs={{1,0},{2,1},{3,2},{5,4},{6,5},{7,6},{9,8},{10,9},{11,10},{13,12},{... | collective-permute-start | bytes 393224 | tf_op jit(solution)/shard_map/ppermute | solution.py:17
  227.5 67.4 %copy-start.9 = (f32[1,1,1,64,1024]{4,3,2,1,0:T(8,128)S(1)}, f32[1,1,1,64,1024]{4,3,2,1,0:T(8,128)}, u32[]{:S(2)}) copy-start(f32[1,1,1,64,1024]{4,3,2,1,0:T(8,128)} %param.15) | copy-start | bytes 786436
  296.2 139.2 %all-gather.15.cloned.1.call-start = ((), (), s32[]{:S(2)}) async-start(), calls=%async_computation.3 | async-start | bytes 4227072 | tf_op jit(solution)/shard_map/all_gather | solution.py:69
  374.6 11.6 %collective-permute-start.12 = (f32[1,256,128]{1,2,0:T(8,128)}, f32[1,256,128]{1,2,0:T(8,128)}, u32[]{:S(2)}, u32[]{:S(2)}) collective-permute-start(f32[1,256,128]{1,2,0:T(8,128)} %bitcast.178), channel_id=1, source_target_pairs={{0,16},{16,32},{32,48},{48,64},{64,80},{80,96},{96,112},{1,17},{17... | collective-permute-start | bytes 393224 | tf_op jit(solution)/shard_map/ppermute | solution.py:16
  377.8 10.7 %collective-permute-start.13 = (f32[1,256,128]{1,2,0:T(8,128)}, f32[1,256,128]{1,2,0:T(8,128)S(1)}, u32[]{:S(2)}, u32[]{:S(2)}) collective-permute-start(f32[1,256,128]{1,2,0:T(8,128)} %bitcast.42), channel_id=1, source_target_pairs={{16,0},{32,16},{48,32},{64,48},{80,64},{96,80},{112,96},{17,1},{33... | collective-permute-start | bytes 393224 | tf_op jit(solution)/shard_map/ppermute | solution.py:17
  380.8 7.7 %collective-permute-start.14 = (f32[1,256,128]{1,2,0:T(8,128)S(1)}, f32[1,256,128]{1,2,0:T(8,128)S(1)}, u32[]{:S(2)}, u32[]{:S(2)}) collective-permute-start(f32[1,256,128]{1,2,0:T(8,128)S(1)} %bitcast.175), channel_id=1, source_target_pairs={{0,4},{4,8},{8,12},{1,5},{5,9},{9,13},{2,6},{6,10},{10,14},{3,7},{... | collective-permute-start | bytes 393224 | tf_op jit(solution)/shard_map/ppermute | solution.py:16
  382.6 7.5 %collective-permute-start.15 = (f32[1,256,128]{1,2,0:T(8,128)S(1)}, f32[1,256,128]{1,2,0:T(8,128)S(1)}, u32[]{:S(2)}, u32[]{:S(2)}) collective-permute-start(f32[1,256,128]{1,2,0:T(8,128)S(1)} %bitcast.172), channel_id=1, source_target_pairs={{4,0},{8,4},{12,8},{5,1},{9,5},{13,9},{6,2},{10,6},{14,10},{7,3},{... | collective-permute-start | bytes 393224 | tf_op jit(solution)/shard_map/ppermute | solution.py:17
  383.9 6.2 %collective-permute-start.16 = (f32[1,256,128]{1,2,0:T(8,128)S(1)}, f32[1,256,128]{1,2,0:T(8,128)S(1)}, u32[]{:S(2)}, u32[]{:S(2)}) collective-permute-start(f32[1,256,128]{1,2,0:T(8,128)S(1)} %bitcast.168), channel_id=1, source_target_pairs={{0,1},{1,2},{2,3},{4,5},{5,6},{6,7},{8,9},{9,10},{10,11},{12,13},{... | collective-permute-start | bytes 393224 | tf_op jit(solution)/shard_map/ppermute | solution.py:16
  386.2 7.2 %collective-permute-start.17 = (f32[1,256,128]{1,2,0:T(8,128)S(1)}, f32[1,256,128]{1,2,0:T(8,128)S(1)}, u32[]{:S(2)}, u32[]{:S(2)}) collective-permute-start(f32[1,256,128]{1,2,0:T(8,128)S(1)} %bitcast.165), channel_id=1, source_target_pairs={{1,0},{2,1},{3,2},{5,4},{6,5},{7,6},{9,8},{10,9},{11,10},{13,12},{... | collective-permute-start | bytes 393224 | tf_op jit(solution)/shard_map/ppermute | solution.py:17
  451.1 46.4 %copy-start.7 = (f32[1024,128]{0,1:T(8,128)}, f32[1024,128]{0,1:T(8,128)S(1)}, u32[]{:S(2)}) copy-start(f32[1024,128]{0,1:T(8,128)S(1)} %get-tuple-element.49) | copy-start | bytes 1572868
  454.1 10.3 %collective-permute-start.18 = (f32[1,256,128]{1,2,0:T(8,128)S(1)}, f32[1,256,128]{1,2,0:T(8,128)S(1)}, u32[]{:S(2)}, u32[]{:S(2)}) collective-permute-start(f32[1,256,128]{1,2,0:T(8,128)S(1)} %bitcast.179), channel_id=1, source_target_pairs={{0,16},{16,32},{32,48},{48,64},{64,80},{80,96},{96,112},{1,17},{17... | collective-permute-start | bytes 393224 | tf_op jit(solution)/shard_map/ppermute | solution.py:16
  456.6 9.8 %collective-permute-start.19 = (f32[1,256,128]{1,2,0:T(8,128)S(1)}, f32[1,256,128]{1,2,0:T(8,128)S(1)}, u32[]{:S(2)}, u32[]{:S(2)}) collective-permute-start(f32[1,256,128]{1,2,0:T(8,128)S(1)} %bitcast.181), channel_id=1, source_target_pairs={{16,0},{32,16},{48,32},{64,48},{80,64},{96,80},{112,96},{17,1},{33... | collective-permute-start | bytes 393224 | tf_op jit(solution)/shard_map/ppermute | solution.py:17
  458.9 8.1 %collective-permute-start.20 = (f32[1,256,128]{1,2,0:T(8,128)S(1)}, f32[1,256,128]{1,2,0:T(8,128)S(1)}, u32[]{:S(2)}, u32[]{:S(2)}) collective-permute-start(f32[1,256,128]{1,2,0:T(8,128)S(1)} %bitcast.176), channel_id=1, source_target_pairs={{0,4},{4,8},{8,12},{1,5},{5,9},{9,13},{2,6},{6,10},{10,14},{3,7},{... | collective-permute-start | bytes 393224 | tf_op jit(solution)/shard_map/ppermute | solution.py:16
  460.8 7.3 %collective-permute-start.21 = (f32[1,256,128]{1,2,0:T(8,128)S(1)}, f32[1,256,128]{1,2,0:T(8,128)S(1)}, u32[]{:S(2)}, u32[]{:S(2)}) collective-permute-start(f32[1,256,128]{1,2,0:T(8,128)S(1)} %bitcast.173), channel_id=1, source_target_pairs={{4,0},{8,4},{12,8},{5,1},{9,5},{13,9},{6,2},{10,6},{14,10},{7,3},{... | collective-permute-start | bytes 393224 | tf_op jit(solution)/shard_map/ppermute | solution.py:17
  462.1 6.7 %collective-permute-start.22 = (f32[1,256,128]{1,2,0:T(8,128)S(1)}, f32[1,256,128]{1,2,0:T(8,128)S(1)}, u32[]{:S(2)}, u32[]{:S(2)}) collective-permute-start(f32[1,256,128]{1,2,0:T(8,128)S(1)} %bitcast.169), channel_id=1, source_target_pairs={{0,1},{1,2},{2,3},{4,5},{5,6},{6,7},{8,9},{9,10},{10,11},{12,13},{... | collective-permute-start | bytes 393224 | tf_op jit(solution)/shard_map/ppermute | solution.py:16
  464.4 7.1 %collective-permute-start.23 = (f32[1,256,128]{1,2,0:T(8,128)S(1)}, f32[1,256,128]{1,2,0:T(8,128)S(1)}, u32[]{:S(2)}, u32[]{:S(2)}) collective-permute-start(f32[1,256,128]{1,2,0:T(8,128)S(1)} %bitcast.166), channel_id=1, source_target_pairs={{1,0},{2,1},{3,2},{5,4},{6,5},{7,6},{9,8},{10,9},{11,10},{13,12},{... | collective-permute-start | bytes 393224 | tf_op jit(solution)/shard_map/ppermute | solution.py:17
  (12 other events, 96.2 us)
Sparse Core Ops, SparseCore 0:
  11.7 70.4 all-gather.8
  92.5 64.3 all-gather.10
  296.4 64.5 all-gather.12
  371.1 64.3 all-gather.14
where the time goes:
time: 577 us; the launch traced here: 576 us
  waiting for transfers between devices  213 us (37%)
  blocking collectives  130 us (23%)
  local copies, waits for them, and re-layouts  106 us (18%)
  matrix products  46.7 us (8%)
  starting transfers between devices  46.4 us (8%)
  other arithmetic  17.1 us (3%)
  between operations  16.5 us (3%)
    all_gather x2, waiting for transfers between devices, body(): lax.all_gather(projected[None], ('gx', 'gy', 'gz'), axis=0, tiled=True)  134 us
    psum x2, blocking collectives, step_totals(): return lax.psum((cross_part, energy_part), ('gx', 'gy', 'gz'))  130 us
    all_gather x2, waiting for transfers between devices, body(): lax.all_gather(solved[None], ('gx', 'gy', 'gz'), axis=0, tiled=True)  69.1 us
    dot_general x8, matrix products, product(): return jnp.dot(left, right, precision=lax.Precision.HIGHEST)  46.7 us
    gather x2, local copies, waits for them, and re-layouts, operate(): picked = whole[links]  41.9 us
    unnamed x81, local copies, waits for them, and re-layouts  31.1 us
    ppermute x12, starting transfers between devices, with_halo(): before = lax.ppermute(last, axis, up)  25.1 us
    ppermute x12, starting transfers between devices, with_halo(): after = lax.ppermute(initial, axis, down)  21.1 us
  transfers between devices with their start and end apart: 28, of which 10 were waited for; matrix products, arithmetic and copies ran while one was open for 7% of the time, Pallas kernels for 0%

commit v1 on v0

v1 whole, which is shorter than its diff:
```python
import jax
import jax.numpy as jnp
from jax import lax
from jax.experimental import pallas as pl
from jax.experimental.pallas import tpu as pltpu
from jax.sharding import PartitionSpec as P

F32 = jnp.float32
BF16 = jnp.bfloat16
MESH = pl.DeviceIdType.MESH

OWN = 1024
NRHS = 128
K = 64
OVR = 256
NEXT = 2560
CHIPS = 64
LCH = 128
NLCH = OWN // LCH
LSLOTS = 4

SHARES = ((0, 24, (2, 1, 0)), (24, 24, (0, 2, 1)), (48, 16, (1, 0, 2)))


def split(x):
    hi = x.astype(BF16)
    lo = (x - hi.astype(F32)).astype(BF16)
    return hi, lo


def put_pair(ref, start, x):
    hi, lo = split(x)
    rows = x.shape[0]
    ref[pl.ds(start, rows), 0:NRHS] = hi
    ref[pl.ds(start, rows), NRHS : 2 * NRHS] = lo


def dot(a, b):
    return jnp.dot(a, b, preferred_element_type=F32)


def dot_nt(a, b):
    return lax.dot_general(a, b, (((1,), (1,)), ((), ())), preferred_element_type=F32)


def fold(p, q):
    return p[:, 0:NRHS] + p[:, NRHS : 2 * NRHS] + q


def stacked(s, x):
    p = dot(s, x)
    half = s.shape[0] // 2
    return fold(p[0:half], p[half:, 0:NRHS])


def ring(v, n):
    return [v] + [lax.rem(v + d, n) for d in range(1, n)]


def kernel(
    rhs_h,
    diag_h,
    couple_h,
    links_h,
    exports_h,
    linv_h,
    basis_h,
    cinv_h,
    owner_s,
    owner_h,
    sol_ref,
    res_ref,
    rv,
    basis_v,
    diag_v,
    couple_v,
    links_v,
    exports_v,
    owner_v,
    lstage,
    linv,
    amat,
    emat,
    cinv_v,
    chl,
    csend,
    crecv,
    gat,
    xg,
    xhl,
    bcat,
    bt,
    bhl,
    msend,
    mrecv,
    l0,
    al0,
    u0,
    w0,
    l1,
    al1,
    gmat,
    hmat,
    sel,
    mhl,
    tcol,
    ncol,
    ecol,
    psrc,
    rbuf,
    sbuf,
    ssend,
    srecv,
    dsend,
    dsis,
    dpair,
    dall,
    in_sem,
    l_sem,
    g_ss,
    g_rs,
    m_ss,
    m_rs,
    c_sem,
    s_sem,
    d_sem,
):
    gx = lax.axis_index("gx")
    y = lax.axis_index("gy")
    z = lax.axis_index("gz")
    x, core = gx // 2, lax.rem(gx, 2)
    chip = (x * 4 + y) * 4 + z
    RX, RY, RZ = ring(x, 4), ring(y, 4), ring(z, 4)
    sister = (x * 2 + 1 - core, y, z)
    place = [x, y, z]

    def at(a, b, c):
        return (a * 2 + core, b, c)

    pending = []

    def send(src, dst, ssem, rsem, device):
        copy = pltpu.make_async_remote_copy(
            src_ref=src, dst_ref=dst, send_sem=ssem, recv_sem=rsem, device_id=device, device_id_type=MESH
        )
        copy.start()
        pending.append(copy)
        return copy

    loads = []
    for i, (src, dst) in enumerate(
        (
            (basis_h, basis_v),
            (rhs_h, rv),
            (exports_h, exports_v),
            (couple_h, couple_v),
            (links_h, links_v),
            (diag_h, diag_v),
            (owner_h, owner_v),
        )
    ):
        copy = pltpu.make_async_copy(src, dst, in_sem.at[i])
        copy.start()
        loads.append(copy)

    def load_columns(t):
        return pltpu.make_async_copy(cinv_h.at[:, pl.ds(pl.multiple_of(t * 128, 128), 128)], cinv_v.at[t], in_sem.at[7])

    def load_column(t, carry):
        load_columns(t).start()
        return carry

    lax.fori_loop(0, 64, load_column, 0)

    def load_chunk(c):
        return pltpu.make_async_copy(linv_h.at[pl.ds(c * LCH, LCH)], lstage.at[c % LSLOTS], l_sem.at[c % LSLOTS])

    for c in range(LSLOTS):
        load_chunk(c).start()

    far = []
    for d in range(1, CHIPS):
        a, b, c = RX[d // 16], RY[(d // 4) % 4], RZ[d % 4]
        far.append(((a * 4 + b) * 4 + c, at(a, b, c)))
    gx_up = (lax.rem(gx + 1, 8), y, z)
    gx_down = (lax.rem(gx + 7, 8), y, z)
    across = (lax.rem(gx + 7 + 2 * core, 8), y, z)
    bar = pltpu.get_barrier_semaphore()
    for _, device in far:
        pl.semaphore_signal(bar, inc=1, device_id=device, device_id_type=MESH)
    pl.semaphore_signal(bar, inc=1, device_id=sister, device_id_type=MESH)
    pl.semaphore_signal(bar, inc=1, device_id=across, device_id_type=MESH)

    def region(buf, order, stage, start, rows):
        index = [slice(None) if a in order[:stage] else place[a] for a in range(3)]
        return buf.at[index[0], index[1], index[2], pl.ds(start, rows), :]

    def along(axis, d):
        p = list(place)
        p[axis] = (RX, RY, RZ)[axis][d]
        return at(*p)

    def gather_start(n, stage):
        for t, (start, rows, order) in enumerate(SHARES):
            reg = region(gat.at[n], order, stage, start, rows)
            for j, d in enumerate((1, 3, 2)):
                send(reg, reg, g_ss.at[n, t, stage, j], g_rs.at[n, t, stage, j], along(order[stage], d))

    def gather_wait(n, stage):
        for t, (start, rows, order) in enumerate(SHARES):
            reg = region(gat.at[n], order, stage, start, rows)
            for j in range(3):
                pltpu.make_async_copy(reg, reg, g_rs.at[n, t, stage, j]).wait()

    steps = (
        (gx_up, gx_down),
        ((gx, RY[1], z), (gx, RY[3], z)),
        ((gx, y, RZ[1]), (gx, y, RZ[3])),
    )
    valid = []
    for coordinate, length in ((gx, 8), (y, 4), (z, 4)):
        valid.append(jnp.where(coordinate > 0, 1.0, 0.0).astype(F32))
        valid.append(jnp.where(coordinate < length - 1, 1.0, 0.0).astype(F32))

    def margins_start(n):
        for e in range(3):
            up, down = steps[e]
            send(msend.at[n, 2 * e + 1], mrecv.at[n, 2 * e], m_ss.at[n, 2 * e], m_rs.at[n, 2 * e], up)
            send(msend.at[n, 2 * e], mrecv.at[n, 2 * e + 1], m_ss.at[n, 2 * e + 1], m_rs.at[n, 2 * e + 1], down)

    def margins_wait(n):
        for b in range(6):
            pltpu.make_async_copy(mrecv.at[n, b], mrecv.at[n, b], m_rs.at[n, b]).wait()

    def outgoing(n):
        def step(d, carry):
            p = dot(emat[pl.ds(pl.multiple_of(d * OVR, OVR), OVR), :], xhl[0:OWN, :])
            msend[n, d] = p[:, 0:NRHS] + p[:, NRHS:]
            return carry

        lax.fori_loop(0, 6, step, 0)

    def import_margins(n):
        margins_wait(n)
        for b in range(6):
            put_pair(xhl, OWN + b * OVR, mrecv[n, b] * valid[b])

    def big_product(mat, dst):
        def step(i, carry):
            r = pl.multiple_of(i * 256, 256)
            p = dot(mat[0, pl.ds(r, 256), :], xhl[...])
            q = dot(mat[1, pl.ds(r, 256), :], xhl[:, 0:NRHS])
            dst[pl.ds(r, 256), :] = fold(p, q)
            return carry

        lax.fori_loop(0, OWN // 256, step, 0)

    def solve(n):
        total = jnp.zeros((256, 256), F32)
        for a in range(4):
            def chunk(b, carry):
                block = gat[n, a, b].reshape(256, NRHS)
                put_pair(xg, pl.multiple_of((a * 4 + b) * 256, 256), block)
                return carry

            lax.fori_loop(0, 4, chunk, 0)
            total = total + dot(chl[:, a * 1024 : (a + 1) * 1024], xg[a * 1024 : (a + 1) * 1024, :])
        res = total[0:128, 0:NRHS] + total[0:128, NRHS:] + total[128:256, 0:NRHS]
        psrc[n, 0] = res[0:64]
        psrc[n, 1] = res[64:128]

    def scatter_start(n):
        for c, device in far:
            copy = pltpu.make_async_remote_copy(
                src_ref=psrc.at[n, :, c, :],
                dst_ref=rbuf.at[n, :, chip, :],
                send_sem=s_sem.at[n, 0],
                recv_sem=s_sem.at[n, 1],
                device_id=device,
                device_id_type=MESH,
            )
            copy.start()
        rbuf[n, :, pl.ds(chip, 1), :] = psrc[n, :, pl.ds(chip, 1), :]

    def wait_all(ref, sem):
        pltpu.make_async_copy(ref, ref, sem).wait()

    def swap(n):
        wait_all(rbuf.at[n, :, pl.ds(0, 63), :], s_sem.at[n, 1])
        send(rbuf.at[n], sbuf.at[n], s_sem.at[n, 2], s_sem.at[n, 3], sister).wait_recv()
        first = rbuf[n, 0] + sbuf[n, 1]
        second = rbuf[n, 1] + sbuf[n, 0]
        hi, lo = split(jnp.concatenate([first, second], axis=0))
        p = dot(sel[...], jnp.concatenate([hi, lo], axis=1))
        ssend[n] = (p[:, 0:NRHS] + p[:, NRHS:]).reshape(CHIPS, 8, NRHS)
        for c, device in far:
            copy = pltpu.make_async_remote_copy(
                src_ref=ssend.at[n, c],
                dst_ref=srecv.at[n, chip],
                send_sem=s_sem.at[n, 4],
                recv_sem=s_sem.at[n, 5],
                device_id=device,
                device_id_type=MESH,
            )
            copy.start()
        srecv[n, chip] = ssend[n, chip]

    def mapped_in(n):
        wait_all(srecv.at[n, pl.ds(0, 63)], s_sem.at[n, 5])
        for s in range(8):
            put_pair(mhl, s * K, srecv[n, :, s, :])

    def scatter_drain(n):
        wait_all(rbuf.at[n, :, pl.ds(0, 63), :], s_sem.at[n, 0])
        wait_all(srecv.at[n, pl.ds(0, 63)], s_sem.at[n, 4])

    def add_coarse(base, dst):
        mine = mhl[6 * K : 7 * K, :]
        dst[...] = base[...] + fold(dot(bt[0], mine), dot(bt[1], mine[:, 0:NRHS]))

    def apply_coarse(base, dst):
        def step(i, carry):
            r = pl.multiple_of(i * 256, 256)
            p = dot(gmat[0, pl.ds(r, 256), :], mhl[...])
            q = dot(gmat[1, pl.ds(r, 256), :], mhl[:, 0:NRHS])
            dst[pl.ds(r, 256), :] = base[pl.ds(r, 256), :] + fold(p, q)
            return carry

        lax.fori_loop(0, OWN // 256, step, 0)

    def totals_start(n, left, right):
        dsend[n] = jnp.zeros((8, NRHS), F32)
        dsend[n, 0:1, :] = jnp.sum(left[...] * right[...], axis=0, keepdims=True)
        dsend[n, 1:2, :] = jnp.sum(right[...] * right[...], axis=0, keepdims=True)
        return send(dsend.at[n], dsis.at[n], d_sem.at[n, 0], d_sem.at[n, 1], sister)

    def totals_spread(n, copy):
        copy.wait_recv()
        dpair[n] = dsend[n] + dsis[n]
        for c, device in far:
            copy = pltpu.make_async_remote_copy(
                src_ref=dpair.at[n, pl.ds(0, 2)],
                dst_ref=dall.at[n, pl.ds(2 * chip, 2)],
                send_sem=d_sem.at[n, 2],
                recv_sem=d_sem.at[n, 3],
                device_id=device,
                device_id_type=MESH,
            )
            copy.start()
        dall[n, pl.ds(2 * chip, 2)] = dpair[n, 0:2]

    def totals_finish(n):
        wait_all(dall.at[n, pl.ds(0, 126)], d_sem.at[n, 3])
        cross = jnp.sum(dall[n, pl.ds(0, 64, stride=2), :], axis=0, keepdims=True)
        energy = jnp.sum(dall[n, pl.ds(1, 64, stride=2), :], axis=0, keepdims=True)
        wait_all(dall.at[n, pl.ds(0, 126)], d_sem.at[n, 2])
        return cross / energy

    loads[0].wait()
    loads[1].wait()
    put_pair(xhl, 0, rv[...])
    hi, lo = split(basis_v[...])
    bhl[0:K, :] = hi
    bhl[K : 2 * K, :] = lo
    gat[0, x, y, z] = stacked(bhl[...], xhl[0:OWN, :])
    pl.semaphore_wait(bar, CHIPS + 1)
    gather_start(0, 0)

    loads[2].wait()
    tcol[...] = jnp.zeros_like(tcol)
    ncol[...] = jnp.zeros_like(ncol)
    tcol[0:6, 0:256] = exports_v[...].astype(F32)
    ecol[...] = tcol[...][:, 0:256].T

    def export_rows(d, carry):
        def group(g, inner):
            rows = ecol[pl.ds(pl.multiple_of(g * 32, 32), 32), :]
            lane = lax.broadcasted_iota(jnp.int32, (32, 8), 1)
            col = jnp.sum(jnp.where(lane == d, rows, 0.0), axis=1, keepdims=True).astype(jnp.int32)
            cells = lax.broadcasted_iota(jnp.int32, (32, OWN), 1)
            emat[pl.ds(pl.multiple_of(d * OVR + g * 32, 32), 32), :] = jnp.where(cells == col, 1.0, 0.0).astype(BF16)
            return inner

        return lax.fori_loop(0, OVR // 32, group, carry)

    lax.fori_loop(0, 6, export_rows, 0)
    outgoing(0)
    margins_start(0)

    pltpu.make_async_copy(cinv_v, cinv_v, in_sem.at[7]).wait()
    lane = lax.broadcasted_iota(jnp.int32, (K, 128), 1)

    def column_block(c, kk, half):
        cx, cy, cz = c // 16, lax.rem(c // 4, 4), lax.rem(c, 4)
        j = owner_s[((cx * 2 + kk) * 4 + cy) * 4 + cz]
        pair = lax.shift_right_logical(j, 1)
        tile = cinv_v[pair]
        turned = pltpu.roll(tile, 64, 1)
        same = jnp.full((K, 128), j - 2 * pair, jnp.int32) == half
        return jnp.where(same, tile, turned)

    def column_pair(m, kk):
        return jnp.where(lane < 64, column_block(2 * m, kk, 0), column_block(2 * m + 1, kk, 1))

    def order_other(m, carry):
        csend[:, pl.ds(pl.multiple_of(m * 128, 128), 128)] = column_pair(m, 1 - core)
        return carry

    def order_mine(m, carry):
        hi, lo = split(column_pair(m, core))
        chl[0:64, pl.ds(pl.multiple_of(m * 128, 128), 128)] = hi
        chl[128:192, pl.ds(pl.multiple_of(m * 128, 128), 128)] = lo
        return carry

    lax.fori_loop(0, 32, order_other, 0)
    ccopy = send(csend, crecv, c_sem.at[0], c_sem.at[1], sister)
    gather_wait(0, 0)
    gather_start(0, 1)
    lax.fori_loop(0, 32, order_mine, 0)

    bcat[0, 0:K, :] = bhl[0:K, :]
    bcat[0, K : 2 * K, :] = bhl[0:K, :]
    bcat[1, 0:K, :] = bhl[K : 2 * K, :]
    bcat[1, K : 2 * K, :] = bhl[K : 2 * K, :]

    def export_basis(d, carry):
        rows = emat[pl.ds(pl.multiple_of(d * OVR, OVR), OVR), :]
        msend[1, d] = dot_nt(rows, bcat[0]) + dot_nt(rows, bcat[1])
        return carry

    lax.fori_loop(0, 6, export_basis, 0)
    gather_wait(0, 1)
    gather_start(0, 2)
    margins_start(1)

    for c in range(NLCH):
        load_chunk(c).wait()

        def halves(g, carry):
            r = pl.multiple_of(g * 16, 16)
            hi, lo = split(lstage[c % LSLOTS, pl.ds(r, 16), :])
            linv[0, pl.ds(c * LCH + r, 16), :] = hi
            linv[1, pl.ds(c * LCH + r, 16), :] = lo
            return carry

        lax.fori_loop(0, LCH // 16, halves, 0)
        if c + LSLOTS < NLCH:
            load_chunk(c + LSLOTS).start()

    import_margins(0)
    big_product(linv, l0)
    put_pair(xhl, 0, l0[...])
    outgoing(2)
    margins_start(2)

    for i in (3, 4, 5):
        loads[i].wait()
    tcol[0:6, :] = couple_v[...]
    tcol[6:7, :] = diag_v[...] + 6.0
    ncol[0:6, :] = links_v[...].astype(F32)
    al0[:, 0:8] = tcol[...].T
    al0[:, 8:16] = ncol[...].T

    def operator_rows(g, carry):
        r = pl.multiple_of(g * 16, 16)
        cols = al0[pl.ds(r, 16), 0:16]
        weights = [cols[:, k : k + 1] for k in range(7)]
        targets = [cols[:, 8 + k : 9 + k].astype(jnp.int32) for k in range(6)]
        own = lax.broadcasted_iota(jnp.int32, (16, 1), 0) + r
        for start in range(0, NEXT, 512):
            cells = lax.broadcasted_iota(jnp.int32, (16, 512), 1) + start
            acc = jnp.zeros((16, 512), F32)
            if start < OWN:
                acc = jnp.where(cells == own, weights[6], 0.0)
            for k in range(6):
                acc = acc - jnp.where(cells == targets[k], weights[k], 0.0)
            hi, lo = split(acc)
            amat[0, pl.ds(r, 16), start : start + 512] = hi
            amat[1, pl.ds(r, 16), start : start + 512] = lo
        return carry

    lax.fori_loop(0, OWN // 16, operator_rows, 0)

    ccopy.wait_recv()

    def sister_rows(m, carry):
        cols = pl.ds(pl.multiple_of(m * 128, 128), 128)
        hi, lo = split(crecv[:, cols])
        chl[64:128, cols] = hi
        chl[192:256, cols] = lo
        return carry

    lax.fori_loop(0, 32, sister_rows, 0)
    gather_wait(0, 2)
    solve(0)
    scatter_start(0)

    margins_wait(1)
    basis_t = basis_v[...].T
    hi, lo = split(basis_t)
    bt[0] = hi
    bt[1] = lo
    hi, lo = split(jnp.concatenate([basis_t, jnp.zeros_like(basis_t)], axis=1))
    xg[0:OWN, 0:128] = hi
    xg[0:OWN, 128:256] = lo
    lane_v = lax.broadcasted_iota(jnp.int32, (OVR, 128), 1)
    for b in range(6):
        mask = jnp.where((lane_v < 64) == (b % 2 == 0), valid[b], 0.0)
        put_pair(xg, OWN + b * OVR, mrecv[1, b] * mask)

    def coarse_columns(i, carry):
        r = pl.multiple_of(i * 256, 256)
        for j in range(4):
            rows = slice(0, OWN) if j == 3 else slice(OWN + j * 512, OWN + (j + 1) * 512)
            p = dot(amat[0, pl.ds(r, 256), rows], xg[rows, :])
            q = dot(amat[1, pl.ds(r, 256), rows], xg[rows, 0:NRHS])
            hi, lo = split(fold(p, q))
            gmat[0, pl.ds(r, 256), j * 128 : (j + 1) * 128] = hi
            gmat[1, pl.ds(r, 256), j * 128 : (j + 1) * 128] = lo
        return carry

    lax.fori_loop(0, OWN // 256, coarse_columns, 0)
    p = dot(bhl[...], gmat[0])
    h = p[0:K] + p[K:] + dot(bhl[0:K, :], gmat[1])
    hi, lo = split(h)
    hmat[0:K, :] = hi
    hmat[K : 2 * K, :] = lo

    loads[6].wait()
    r_ = lax.broadcasted_iota(jnp.int32, (512, 128), 0)
    q_ = lax.broadcasted_iota(jnp.int32, (512, 128), 1)
    c_, s_ = r_ // 8, r_ % 8
    dx = jnp.where(s_ == 0, 7, jnp.where(s_ == 1, 1, 0))
    dy = jnp.where(s_ == 2, 3, jnp.where(s_ == 3, 1, 0))
    dz = jnp.where(s_ == 4, 3, jnp.where(s_ == 5, 1, 0))
    px = ((c_ // 16) * 2 + core + dx) % 8
    py = ((c_ // 4) % 4 + dy) % 4
    pz = (c_ % 4 + dz) % 4
    wanted = jnp.where(q_ == (px * 4 + py) * 4 + pz, 1.0, 0.0).astype(BF16)
    i_ = lax.broadcasted_iota(jnp.int32, (128, 128), 0)
    ch_ = i_ % 64
    kk_ = (core + i_ // 64) % 2
    block = (((ch_ // 16) * 2 + kk_) * 4 + (ch_ // 4) % 4) * 4 + ch_ % 4
    held = jnp.where(owner_v[...] == block, 1.0, 0.0).astype(BF16)
    sel[...] = dot_nt(wanted, held).astype(BF16)

    swap(0)
    import_margins(2)
    big_product(amat, al0)
    put_pair(xhl, 0, al0[...])
    projected = stacked(bhl[...], xhl[0:OWN, :])
    mapped_in(0)

    gat[1, x, y, z] = projected + stacked(hmat[...], mhl[...])
    gather_start(1, 0)
    apply_coarse(al0, w0)
    put_pair(xhl, 0, w0[...])
    outgoing(3)
    margins_start(3)
    dots = totals_start(0, rv, w0)
    gather_wait(1, 0)
    gather_start(1, 1)
    totals_spread(0, dots)
    add_coarse(l0, u0)
    gather_wait(1, 1)
    gather_start(1, 2)
    import_margins(3)
    big_product(linv, l1)
    put_pair(xhl, 0, l1[...])
    outgoing(4)
    margins_start(4)
    alpha0 = totals_finish(0)
    rv[...] = rv[...] - alpha0 * w0[...]
    import_margins(4)
    big_product(amat, al1)
    gather_wait(1, 2)
    solve(1)
    scatter_start(1)
    swap(1)
    mapped_in(1)
    apply_coarse(al1, al1)
    w0[...] = w0[...] - alpha0 * al1[...]
    dots = totals_start(1, rv, w0)
    totals_spread(1, dots)
    add_coarse(l1, l1)
    l1[...] = u0[...] - alpha0 * l1[...]
    alpha1 = totals_finish(1)
    sol_ref[...] = alpha0 * u0[...] + alpha1 * l1[...]
    res_ref[...] = rv[...] - alpha1 * w0[...]

    for copy in pending:
        copy.wait_send()
    scatter_drain(0)
    scatter_drain(1)


def run(rhs, diagonal, couple, links, exports, linv, basis, cinv, owner):
    field = (OWN, NRHS)
    dma = pltpu.SemaphoreType.DMA
    vm = pltpu.VMEM
    scratch = [
        vm(field, F32),
        vm((K, OWN), F32),
        vm((1, OWN), F32),
        vm((6, OWN), F32),
        vm((6, OWN), jnp.int32),
        vm((6, OVR), jnp.int32),
        vm((1, 128), jnp.int32),
        vm((LSLOTS, LCH, NEXT), F32),
        vm((2, OWN, NEXT), BF16),
        vm((2, OWN, NEXT), BF16),
        vm((6 * OVR, OWN), BF16),
        vm((64, K, 128), F32),
        vm((256, 4096), BF16),
        vm((K, 4096), F32),
        vm((K, 4096), F32),
        vm((2, 4, 4, 4, K, NRHS), F32),
        vm((4096, 256), BF16),
        vm((NEXT, 256), BF16),
        vm((2, 128, OWN), BF16),
        vm((2, OWN, K), BF16),
        vm((128, OWN), BF16),
        vm((5, 6, OVR, NRHS), F32),
        vm((5, 6, OVR, NRHS), F32),
        vm(field, F32),
        vm(field, F32),
        vm(field, F32),
        vm(field, F32),
        vm(field, F32),
        vm(field, F32),
        vm((2, OWN, 512), BF16),
        vm((128, 512), BF16),
        vm((512, 128), BF16),
        vm((512, 256), BF16),
        vm((8, OWN), F32),
        vm((8, OWN), F32),
        vm((OVR, 8), F32),
        vm((2, 2, CHIPS, NRHS), F32),
        vm((2, 2, CHIPS, NRHS), F32),
        vm((2, 2, CHIPS, NRHS), F32),
        vm((2, CHIPS, 8, NRHS), F32),
        vm((2, CHIPS, 8, NRHS), F32),
        vm((2, 8, NRHS), F32),
        vm((2, 8, NRHS), F32),
        vm((2, 8, NRHS), F32),
        vm((2, 128, NRHS), F32),
        dma((8,)),
        dma((LSLOTS,)),
        dma((2, 3, 3, 3)),
        dma((2, 3, 3, 3)),
        dma((5, 6)),
        dma((5, 6)),
        dma((2,)),
        dma((2, 6)),
        dma((2, 4)),
    ]
    anywhere = pl.BlockSpec(memory_space=pl.ANY)
    return pl.pallas_call(
        kernel,
        out_shape=(jax.ShapeDtypeStruct(field, F32), jax.ShapeDtypeStruct(field, F32)),
        in_specs=[anywhere] * 8 + [pl.BlockSpec(memory_space=pltpu.SMEM), anywhere],
        out_specs=(pl.BlockSpec(memory_space=pltpu.VMEM), pl.BlockSpec(memory_space=pltpu.VMEM)),
        scratch_shapes=scratch,
        compiler_params=pltpu.CompilerParams(
            collective_id=0, has_side_effects=True, vmem_limit_bytes=63 * 1024 * 1024
        ),
        cost_estimate=pl.CostEstimate(flops=12_000_000_000, bytes_accessed=15_000_000, transcendentals=0),
    )(rhs, diagonal, couple, links, exports, linv, basis, cinv, owner, owner.reshape(1, 128))


def body(rhs, diagonal, couple, neighbours, export_rows, local_inverse, basis, coarse_inverse, owner):
    solution, residual = run(
        rhs.reshape(OWN, NRHS),
        diagonal.reshape(1, OWN),
        couple.reshape(6, OWN),
        neighbours.reshape(6, OWN),
        export_rows.reshape(6, OVR),
        local_inverse.reshape(OWN, NEXT),
        basis.reshape(K, OWN),
        coarse_inverse,
        owner,
    )
    return solution.reshape(rhs.shape), residual.reshape(rhs.shape)


def solution(mesh):
    placed = (
        P("gx", "gy", "gz", None, None),
        P("gx", "gy", "gz", None),
        P("gx", "gy", "gz", None, None),
        P("gx", "gy", "gz", None, None),
        P("gx", "gy", "gz", None, None),
        P("gx", "gy", "gz", None, None),
        P("gx", "gy", "gz", None, None),
        P(("gx", "gy", "gz"), None),
        P(),
    )
    return jax.shard_map(
        body,
        mesh=mesh,
        in_specs=placed,
        out_specs=(P("gx", "gy", "gz", None, None), P("gx", "gy", "gz", None, None)),
        check_vma=False,
    )
```

time: 577 us -> 133 us (0.23)
  waiting for transfers between devices: 213 us -> 0 us
  blocking collectives: 130 us -> 0 us
  Pallas kernels: 0 us -> 124 us
  local copies, waits for them, and re-layouts: 106 us -> 7.74 us
  matrix products: 46.7 us -> 0 us
  starting transfers between devices: 46.4 us -> 0 us
  other arithmetic: 17.1 us -> 0 us
  between operations: 16.5 us -> 0.64 us
    all_gather x4 -> x0, waiting for transfers between devices: 203 us -> none  [the longest x2 134 us: body(): lax.all_gather(projected[None], ('gx', 'gy', 'gz'), axis=0, tiled=True)]
    psum x2 -> x0, blocking collectives: 130 us -> none  [step_totals(): return lax.psum((cross_part, energy_part), ('gx', 'gy', 'gz'))]
    pallas_call x0 -> x1, Pallas kernels: none -> 124 us  [run(): pl.pallas_call(kernel, out_shape=(jax.ShapeDtypeStruct(field, F32), jax.S...]
    gather x8 -> x0, local copies, waits for them, and re-layouts: 63.3 us -> none  [the longest x2 41.9 us: operate(): picked = whole[links]]
    dot_general x8 -> x0, matrix products: 46.7 us -> none  [product(): return jnp.dot(left, right, precision=lax.Precision.HIGHEST)]
    ppermute x24 -> x0, starting transfers between devices: 46.2 us -> none  [the longest x12 25.1 us: with_halo(): before = lax.ppermute(last, axis, up)]
    unnamed x81 -> x5, local copies, waits for them, and re-layouts: 31.1 us -> 7.74 us
    ppermute x24 -> x0, waiting for transfers between devices: 9.65 us -> none  [the longest x12 9.62 us: with_halo(): after = lax.ppermute(initial, axis, down)]
  transfers between devices with their start and end apart: 28 -> 0, of which waited for: 10 -> 0; matrix products, arithmetic and copies ran while one was open for 7% -> 0% of each run, Pallas kernels for 0% -> 0%
where the time goes in v1:
time: 133 us
  Pallas kernels  124 us (93%)
  local copies, waits for them, and re-layouts  7.74 us (6%)
    pallas_call x1, Pallas kernels, run(): pl.pallas_call(kernel, out_shape=(jax.ShapeDtypeStruct(field, F32), jax.S...  124 us
    unnamed x5, local copies, waits for them, and re-layouts  7.74 us

profile of v1, /device:TPU:1, one launch (start us, length us, event | category | flops | bytes accessed | tf_op | source)
XLA Modules:
  0.0 132.7 jit_solution(6305248529605784138)
XLA Ops:
  0.6 1.3 copy.19
  1.9 1.4 %copy.18 = f32[1,1,1,6,1024]{4,3,2,1,0:T(8,128)} copy(f32[1,1,1,6,1024]{4,2,3,1,0:T(1,128)} %param.11) | data formatting | bytes 49152
  3.3 1.4 %copy.17 = s32[1,1,1,6,1024]{4,3,2,1,0:T(8,128)} copy(s32[1,1,1,6,1024]{4,2,3,1,0:T(1,128)} %param.12) | data formatting | bytes 49152
  4.6 124.3 %shard_map.104 = (f32[1024,128]{1,0:T(8,128)}, f32[1024,128]{1,0:T(8,128)}) custom-call(f32[1024,128]{1,0:T(8,128)} %bitcast.22, f32[1,1024]{1,0:T(1,128)} %bitcast.24, f32[6,1024]{1,0:T(8,128)} %bitcast.18, s32[6,1024]{1,0:T(8,128)} %bitcast.19, s32[6,256]{1,0:T(8,128)} %bitcast.20, f32[1024,2560]{1,0:T(8,128)} %bitcast.21, f32[64,1024]{1,0:T(8,128)} %bitcast.23, ...), custom_call_target="tpu_custom_call" | custom-call | flops 12000000000 | bytes 15000000 | tf_op jit(solution)/shard_map/pallas_call | solution.py:658
  128.9 1.9 %copy.22 = f32[1,1,1,1024,128]{4,3,2,1,0:T(8,128)} copy(f32[1,1,1,1024,128]{4,3,2,1,0:T(8,128)} %bitcast.17) | data formatting | bytes 1048576
  130.8 1.9 %copy.23 = f32[1,1,1,1024,128]{4,3,2,1,0:T(8,128)} copy(f32[1,1,1,1024,128]{4,3,2,1,0:T(8,128)} %bitcast.16) | data formatting | bytes 1048576

commit v2 on v1

--- a/solution.py
+++ b/solution.py
@@ -55,6 +55,10 @@
 
 def ring(v, n):
     return [v] + [lax.rem(v + d, n) for d in range(1, n)]
+
+
+def hops(d):
+    return sum((0, 1, 2, 1)[i] for i in (d // 16, (d // 4) % 4, d % 4))
 
 
 def kernel(
@@ -69,7 +73,10 @@
     owner_s,
     owner_h,
     sol_ref,
+    update_ref,
     res_ref,
+    image_ref,
+    alpha_ref,
     rv,
     basis_v,
     diag_v,
@@ -93,6 +100,8 @@
     bhl,
     msend,
     mrecv,
+    bsend,
+    brecv,
     l0,
     al0,
     u0,
@@ -124,6 +133,7 @@
     c_sem,
     s_sem,
     d_sem,
+    out_sem,
 ):
     gx = lax.axis_index("gx")
     y = lax.axis_index("gy")
@@ -136,6 +146,11 @@
 
     def at(a, b, c):
         return (a * 2 + core, b, c)
+
+    def along(axis, d):
+        p = list(place)
+        p[axis] = (RX, RY, RZ)[axis][d]
+        return at(*p)
 
     pending = []
 
@@ -179,38 +194,54 @@
         load_chunk(c).start()
 
     far = []
-    for d in range(1, CHIPS):
+    for d in sorted(range(1, CHIPS), key=hops, reverse=True):
         a, b, c = RX[d // 16], RY[(d // 4) % 4], RZ[d % 4]
         far.append(((a * 4 + b) * 4 + c, at(a, b, c)))
     gx_up = (lax.rem(gx + 1, 8), y, z)
     gx_down = (lax.rem(gx + 7, 8), y, z)
     across = (lax.rem(gx + 7 + 2 * core, 8), y, z)
     bar = pltpu.get_barrier_semaphore()
-    for _, device in far:
+    near = [along(axis, d) for d in (2, 1, 3) for axis in range(3)] + [across, sister]
+    for device in near:
         pl.semaphore_signal(bar, inc=1, device_id=device, device_id_type=MESH)
-    pl.semaphore_signal(bar, inc=1, device_id=sister, device_id_type=MESH)
-    pl.semaphore_signal(bar, inc=1, device_id=across, device_id_type=MESH)
-
-    def region(buf, order, stage, start, rows):
+
+    def region(n, t, stage, line=0):
+        start, rows, order = SHARES[t]
         index = [slice(None) if a in order[:stage] else place[a] for a in range(3)]
-        return buf.at[index[0], index[1], index[2], pl.ds(start, rows), :]
-
-    def along(axis, d):
-        p = list(place)
-        p[axis] = (RX, RY, RZ)[axis][d]
-        return at(*p)
-
-    def gather_start(n, stage):
-        for t, (start, rows, order) in enumerate(SHARES):
-            reg = region(gat.at[n], order, stage, start, rows)
+        if stage == 2:
+            axis = order[1]
+            index[axis] = (RX, RY, RZ)[axis][line]
+        return gat.at[n].at[index[0], index[1], index[2], pl.ds(start, rows), :]
+
+    def gather_send(n, stage, line=0):
+        slot = stage + line
+        for t in range(3):
+            reg = region(n, t, stage, line)
             for j, d in enumerate((1, 3, 2)):
-                send(reg, reg, g_ss.at[n, t, stage, j], g_rs.at[n, t, stage, j], along(order[stage], d))
-
-    def gather_wait(n, stage):
-        for t, (start, rows, order) in enumerate(SHARES):
-            reg = region(gat.at[n], order, stage, start, rows)
+                send(reg, reg, g_ss.at[n, t, slot, j], g_rs.at[n, t, slot, j], along(SHARES[t][2][stage], d))
+
+    def gather_recv(n, stage, line=0):
+        for t in range(3):
+            reg = region(n, t, stage, line)
             for j in range(3):
-                pltpu.make_async_copy(reg, reg, g_rs.at[n, t, stage, j]).wait()
+                pltpu.make_async_copy(reg, reg, g_rs.at[n, t, stage + line, j]).wait()
+
+    def gather_one(n):
+        gather_send(n, 0)
+
+    def gather_two(n):
+        gather_recv(n, 0)
+        gather_send(n, 1)
+        gather_send(n, 2, 0)
+
+    def gather_three(n):
+        gather_recv(n, 1)
+        for line in (1, 3, 2):
+            gather_send(n, 2, line)
+
+    def gather_done(n):
+        for line in (0, 1, 3, 2):
+            gather_recv(n, 2, line)
 
     steps = (
         (gx_up, gx_down),
@@ -222,48 +253,52 @@
         valid.append(jnp.where(coordinate > 0, 1.0, 0.0).astype(F32))
         valid.append(jnp.where(coordinate < length - 1, 1.0, 0.0).astype(F32))
 
+    def margins(n):
+        return (bsend, brecv) if n == 1 else (msend.at[n if n == 0 else n - 1], mrecv.at[n if n == 0 else n - 1])
+
     def margins_start(n):
+        out, into = margins(n)
         for e in range(3):
             up, down = steps[e]
-            send(msend.at[n, 2 * e + 1], mrecv.at[n, 2 * e], m_ss.at[n, 2 * e], m_rs.at[n, 2 * e], up)
-            send(msend.at[n, 2 * e], mrecv.at[n, 2 * e + 1], m_ss.at[n, 2 * e + 1], m_rs.at[n, 2 * e + 1], down)
+            send(out.at[2 * e + 1], into.at[2 * e], m_ss.at[n, 2 * e], m_rs.at[n, 2 * e], up)
+            send(out.at[2 * e], into.at[2 * e + 1], m_ss.at[n, 2 * e + 1], m_rs.at[n, 2 * e + 1], down)
 
     def margins_wait(n):
+        into = margins(n)[1]
         for b in range(6):
-            pltpu.make_async_copy(mrecv.at[n, b], mrecv.at[n, b], m_rs.at[n, b]).wait()
+            pltpu.make_async_copy(into.at[b], into.at[b], m_rs.at[n, b]).wait()
 
     def outgoing(n):
+        out = margins(n)[0]
+
         def step(d, carry):
             p = dot(emat[pl.ds(pl.multiple_of(d * OVR, OVR), OVR), :], xhl[0:OWN, :])
-            msend[n, d] = p[:, 0:NRHS] + p[:, NRHS:]
+            out[d] = p[:, 0:NRHS] + p[:, NRHS:]
             return carry
 
         lax.fori_loop(0, 6, step, 0)
 
     def import_margins(n):
         margins_wait(n)
+        into = margins(n)[1]
         for b in range(6):
-            put_pair(xhl, OWN + b * OVR, mrecv[n, b] * valid[b])
+            put_pair(xhl, OWN + b * OVR, into[b] * valid[b])
 
     def big_product(mat, dst):
         def step(i, carry):
-            r = pl.multiple_of(i * 256, 256)
-            p = dot(mat[0, pl.ds(r, 256), :], xhl[...])
-            q = dot(mat[1, pl.ds(r, 256), :], xhl[:, 0:NRHS])
-            dst[pl.ds(r, 256), :] = fold(p, q)
+            r = pl.multiple_of(i * 512, 512)
+            p = dot(mat[0, pl.ds(r, 512), :], xhl[...])
+            q = dot(mat[1, pl.ds(r, 512), :], xhl[:, 0:NRHS])
+            dst[pl.ds(r, 512), :] = fold(p, q)
             return carry
 
-        lax.fori_loop(0, OWN // 256, step, 0)
+        lax.fori_loop(0, OWN // 512, step, 0)
 
     def solve(n):
         total = jnp.zeros((256, 256), F32)
         for a in range(4):
-            def chunk(b, carry):
-                block = gat[n, a, b].reshape(256, NRHS)
-                put_pair(xg, pl.multiple_of((a * 4 + b) * 256, 256), block)
-                return carry
-
-            lax.fori_loop(0, 4, chunk, 0)
+            for b in range(4):
+                put_pair(xg, (a * 4 + b) * 256, gat[n, a, b].reshape(256, NRHS))
             total = total + dot(chl[:, a * 1024 : (a + 1) * 1024], xg[a * 1024 : (a + 1) * 1024, :])
         res = total[0:128, 0:NRHS] + total[0:128, NRHS:] + total[128:256, 0:NRHS]
         psrc[n, 0] = res[0:64]
@@ -295,24 +330,24 @@
         ssend[n] = (p[:, 0:NRHS] + p[:, NRHS:]).reshape(CHIPS, 8, NRHS)
         for c, device in far:
             copy = pltpu.make_async_remote_copy(
-                src_ref=ssend.at[n, c],
-                dst_ref=srecv.at[n, chip],
+                src_ref=ssend.at[n, c, pl.ds(0, 7)],
+                dst_ref=srecv.at[n, chip, pl.ds(0, 7)],
                 send_sem=s_sem.at[n, 4],
                 recv_sem=s_sem.at[n, 5],
                 device_id=device,
                 device_id_type=MESH,
             )
             copy.start()
-        srecv[n, chip] = ssend[n, chip]
+        srecv[n, chip, 0:7] = ssend[n, chip, 0:7]
 
     def mapped_in(n):
-        wait_all(srecv.at[n, pl.ds(0, 63)], s_sem.at[n, 5])
-        for s in range(8):
+        wait_all(srecv.at[n, pl.ds(0, 63), pl.ds(0, 7)], s_sem.at[n, 5])
+        for s in range(7):
             put_pair(mhl, s * K, srecv[n, :, s, :])
 
     def scatter_drain(n):
         wait_all(rbuf.at[n, :, pl.ds(0, 63), :], s_sem.at[n, 0])
-        wait_all(srecv.at[n, pl.ds(0, 63)], s_sem.at[n, 4])
+        wait_all(srecv.at[n, pl.ds(0, 63), pl.ds(0, 7)], s_sem.at[n, 4])
 
     def add_coarse(base, dst):
         mine = mhl[6 * K : 7 * K, :]
@@ -356,6 +391,7 @@
         wait_all(dall.at[n, pl.ds(0, 126)], d_sem.at[n, 2])
         return cross / energy
 
+    mhl[7 * K :, :] = jnp.zeros((K, 2 * NRHS), BF16)
     loads[0].wait()
     loads[1].wait()
     put_pair(xhl, 0, rv[...])
@@ -363,14 +399,13 @@
     bhl[0:K, :] = hi
     bhl[K : 2 * K, :] = lo
     gat[0, x, y, z] = stacked(bhl[...], xhl[0:OWN, :])
-    pl.semaphore_wait(bar, CHIPS + 1)
-    gather_start(0, 0)
 
     loads[2].wait()
     tcol[...] = jnp.zeros_like(tcol)
     ncol[...] = jnp.zeros_like(ncol)
-    tcol[0:6, 0:256] = exports_v[...].astype(F32)
-    ecol[...] = tcol[...][:, 0:256].T
+    for d in range(6):
+        tcol[d : d + 1, 0:OVR] = exports_v[d].astype(F32)
+    ecol[...] = tcol[...][:, 0:OVR].T
 
     def export_rows(d, carry):
         def group(g, inner):
@@ -384,8 +419,6 @@
         return lax.fori_loop(0, OVR // 32, group, carry)
 
     lax.fori_loop(0, 6, export_rows, 0)
-    outgoing(0)
-    margins_start(0)
 
     pltpu.make_async_copy(cinv_v, cinv_v, in_sem.at[7]).wait()
     lane = lax.broadcasted_iota(jnp.int32, (K, 128), 1)
@@ -413,25 +446,62 @@
         return carry
 
     lax.fori_loop(0, 32, order_other, 0)
+
+    for i in (3, 4, 5):
+        loads[i].wait()
+    own_row = lax.broadcasted_iota(jnp.int32, (1, OWN), 1)
+    targets = [links_v[k] for k in range(6)]
+    weights = [couple_v[k] for k in range(6)]
+    centre = diag_v[...] + 6.0
+    for k in range(6):
+        centre = centre - jnp.where(targets[k] == own_row, weights[k], 0.0)
+        gone = targets[k] == own_row
+        total = weights[k]
+        for m in range(6):
+            if m < k:
+                gone = gone | (targets[m] == targets[k])
+            if m > k:
+                total = total + jnp.where(targets[m] == targets[k], weights[m], 0.0)
+        tcol[k : k + 1, :] = -total
+        ncol[k : k + 1, :] = jnp.where(gone, -1, targets[k]).astype(F32)
+    tcol[6:7, :] = centre
+    ncol[6:7, :] = own_row.astype(F32)
+    al0[:, 0:8] = tcol[...].T
+    al0[:, 8:16] = ncol[...].T
+
+    def operator_rows(g, carry):
+        r = pl.multiple_of(g * 16, 16)
+        cols = al0[pl.ds(r, 16), 0:16]
+        values = [split(jnp.broadcast_to(cols[:, k : k + 1], (16, 128))) for k in range(7)]
+        places = [
+            jnp.broadcast_to(cols[:, 8 + k : 9 + k], (16, 128)).astype(jnp.int32).astype(jnp.int16) for k in range(7)
+        ]
+        lanes = lax.broadcasted_iota(jnp.int32, (16, 128), 1)
+        for j in range(NEXT // 128):
+            cells = (lanes + j * 128).astype(jnp.int16)
+            hi = jnp.zeros((16, 128), BF16)
+            lo = jnp.zeros((16, 128), BF16)
+            for k in range(7 if j < OWN // 128 else 6):
+                hit = cells == places[k]
+                hi = jnp.where(hit, values[k][0], hi)
+                lo = jnp.where(hit, values[k][1], lo)
+            amat[0, pl.ds(r, 16), j * 128 : (j + 1) * 128] = hi
+            amat[1, pl.ds(r, 16), j * 128 : (j + 1) * 128] = lo
+        return carry
+
+    def build_operator(first, last):
+        lax.fori_loop(first, last, operator_rows, 0)
+
+    pl.semaphore_wait(bar, len(near))
+    gather_one(0)
     ccopy = send(csend, crecv, c_sem.at[0], c_sem.at[1], sister)
-    gather_wait(0, 0)
-    gather_start(0, 1)
+    outgoing(0)
+    margins_start(0)
+    build_operator(0, 6)
+    gather_two(0)
     lax.fori_loop(0, 32, order_mine, 0)
-
-    bcat[0, 0:K, :] = bhl[0:K, :]
-    bcat[0, K : 2 * K, :] = bhl[0:K, :]
-    bcat[1, 0:K, :] = bhl[K : 2 * K, :]
-    bcat[1, K : 2 * K, :] = bhl[K : 2 * K, :]
-
-    def export_basis(d, carry):
-        rows = emat[pl.ds(pl.multiple_of(d * OVR, OVR), OVR), :]
-        msend[1, d] = dot_nt(rows, bcat[0]) + dot_nt(rows, bcat[1])
-        return carry
-
-    lax.fori_loop(0, 6, export_basis, 0)
-    gather_wait(0, 1)
-    gather_start(0, 2)
-    margins_start(1)
+    build_operator(6, 18)
+    gather_three(0)
 
     for c in range(NLCH):
         load_chunk(c).wait()
@@ -451,36 +521,21 @@
     big_product(linv, l0)
     put_pair(xhl, 0, l0[...])
     outgoing(2)
-    margins_start(2)
-
-    for i in (3, 4, 5):
-        loads[i].wait()
-    tcol[0:6, :] = couple_v[...]
-    tcol[6:7, :] = diag_v[...] + 6.0
-    ncol[0:6, :] = links_v[...].astype(F32)
-    al0[:, 0:8] = tcol[...].T
-    al0[:, 8:16] = ncol[...].T
-
-    def operator_rows(g, carry):
-        r = pl.multiple_of(g * 16, 16)
-        cols = al0[pl.ds(r, 16), 0:16]
-        weights = [cols[:, k : k + 1] for k in range(7)]
-        targets = [cols[:, 8 + k : 9 + k].astype(jnp.int32) for k in range(6)]
-        own = lax.broadcasted_iota(jnp.int32, (16, 1), 0) + r
-        for start in range(0, NEXT, 512):
-            cells = lax.broadcasted_iota(jnp.int32, (16, 512), 1) + start
-            acc = jnp.zeros((16, 512), F32)
-            if start < OWN:
-                acc = jnp.where(cells == own, weights[6], 0.0)
-            for k in range(6):
-                acc = acc - jnp.where(cells == targets[k], weights[k], 0.0)
-            hi, lo = split(acc)
-            amat[0, pl.ds(r, 16), start : start + 512] = hi
-            amat[1, pl.ds(r, 16), start : start + 512] = lo
+    build_operator(18, 40)
+
+    bcat[0, 0:K, :] = bhl[0:K, :]
+    bcat[0, K : 2 * K, :] = bhl[0:K, :]
+    bcat[1, 0:K, :] = bhl[K : 2 * K, :]
+    bcat[1, K : 2 * K, :] = bhl[K : 2 * K, :]
+    lane_h = lax.broadcasted_iota(jnp.int32, (128, 128), 1)
+
+    def export_basis(d, carry):
+        rows = emat[pl.ds(pl.multiple_of(d * OVR, OVR), OVR), :]
+        p = dot_nt(rows, bcat[0]) + dot_nt(rows, bcat[1])
+        bsend[d] = jnp.where(lane_h < 64, p[0:128], p[128:256])
         return carry
 
-    lax.fori_loop(0, OWN // 16, operator_rows, 0)
-
+    lax.fori_loop(0, 6, export_basis, 0)
     ccopy.wait_recv()
 
     def sister_rows(m, carry):
@@ -491,40 +546,12 @@
         return carry
 
     lax.fori_loop(0, 32, sister_rows, 0)
-    gather_wait(0, 2)
+    gather_done(0)
+    margins_start(2)
+    margins_start(1)
     solve(0)
     scatter_start(0)
-
-    margins_wait(1)
-    basis_t = basis_v[...].T
-    hi, lo = split(basis_t)
-    bt[0] = hi
-    bt[1] = lo
-    hi, lo = split(jnp.concatenate([basis_t, jnp.zeros_like(basis_t)], axis=1))
-    xg[0:OWN, 0:128] = hi
-    xg[0:OWN, 128:256] = lo
-    lane_v = lax.broadcasted_iota(jnp.int32, (OVR, 128), 1)
-    for b in range(6):
-        mask = jnp.where((lane_v < 64) == (b % 2 == 0), valid[b], 0.0)
-        put_pair(xg, OWN + b * OVR, mrecv[1, b] * mask)
-
-    def coarse_columns(i, carry):
-        r = pl.multiple_of(i * 256, 256)
-        for j in range(4):
-            rows = slice(0, OWN) if j == 3 else slice(OWN + j * 512, OWN + (j + 1) * 512)
-            p = dot(amat[0, pl.ds(r, 256), rows], xg[rows, :])
-            q = dot(amat[1, pl.ds(r, 256), rows], xg[rows, 0:NRHS])
-            hi, lo = split(fold(p, q))
-            gmat[0, pl.ds(r, 256), j * 128 : (j + 1) * 128] = hi
-            gmat[1, pl.ds(r, 256), j * 128 : (j + 1) * 128] = lo
-        return carry
-
-    lax.fori_loop(0, OWN // 256, coarse_columns, 0)
-    p = dot(bhl[...], gmat[0])
-    h = p[0:K] + p[K:] + dot(bhl[0:K, :], gmat[1])
-    hi, lo = split(h)
-    hmat[0:K, :] = hi
-    hmat[K : 2 * K, :] = lo
+    build_operator(40, 64)
 
     loads[6].wait()
     r_ = lax.broadcasted_iota(jnp.int32, (512, 128), 0)
@@ -543,55 +570,98 @@
     block = (((ch_ // 16) * 2 + kk_) * 4 + (ch_ // 4) % 4) * 4 + ch_ % 4
     held = jnp.where(owner_v[...] == block, 1.0, 0.0).astype(BF16)
     sel[...] = dot_nt(wanted, held).astype(BF16)
-
     swap(0)
+
     import_margins(2)
     big_product(amat, al0)
     put_pair(xhl, 0, al0[...])
     projected = stacked(bhl[...], xhl[0:OWN, :])
+
+    margins_wait(1)
+    basis_t = basis_v[...].T
+    hi, lo = split(basis_t)
+    bt[0] = hi
+    bt[1] = lo
+    hi, lo = split(jnp.concatenate([basis_t, jnp.zeros_like(basis_t)], axis=1))
+    xg[0:OWN, 0:128] = hi
+    xg[0:OWN, 128:256] = lo
+    for b in range(6):
+        mask = jnp.where((lane_h < 64) == (b % 2 == 0), valid[b], 0.0)
+        top, bottom = brecv[b], pltpu.roll(brecv[b], 64, 1)
+        if b % 2 == 1:
+            top, bottom = bottom, top
+        put_pair(xg, OWN + b * OVR, top * mask)
+        put_pair(xg, OWN + b * OVR + 128, bottom * mask)
+
+    def coarse_columns(i, carry):
+        r = pl.multiple_of(i * 256, 256)
+        for j in range(4):
+            rows = slice(0, OWN) if j == 3 else slice(OWN + j * 512, OWN + (j + 1) * 512)
+            p = dot(amat[0, pl.ds(r, 256), rows], xg[rows, :])
+            q = dot(amat[1, pl.ds(r, 256), rows], xg[rows, 0:NRHS])
+            hi, lo = split(fold(p, q))
+            gmat[0, pl.ds(r, 256), j * 128 : (j + 1) * 128] = hi
+            gmat[1, pl.ds(r, 256), j * 128 : (j + 1) * 128] = lo
+        return carry
+
+    lax.fori_loop(0, OWN // 256, coarse_columns, 0)
+    p = dot(bhl[...], gmat[0])
+    h = p[0:K] + p[K:] + dot(bhl[0:K, :], gmat[1])
+    hi, lo = split(h)
+    hmat[0:K, :] = hi
+    hmat[K : 2 * K, :] = lo
+
     mapped_in(0)
 
     gat[1, x, y, z] = projected + stacked(hmat[...], mhl[...])
-    gather_start(1, 0)
+    gather_one(1)
     apply_coarse(al0, w0)
     put_pair(xhl, 0, w0[...])
     outgoing(3)
+    gather_two(1)
     margins_start(3)
     dots = totals_start(0, rv, w0)
-    gather_wait(1, 0)
-    gather_start(1, 1)
+    add_coarse(l0, u0)
+    gather_three(1)
     totals_spread(0, dots)
-    add_coarse(l0, u0)
-    gather_wait(1, 1)
-    gather_start(1, 2)
     import_margins(3)
     big_product(linv, l1)
     put_pair(xhl, 0, l1[...])
     outgoing(4)
-    margins_start(4)
     alpha0 = totals_finish(0)
     rv[...] = rv[...] - alpha0 * w0[...]
+    first = pltpu.make_async_copy(rv, res_ref, out_sem.at[0])
+    first.start()
+    gather_done(1)
+    margins_start(4)
+    solve(1)
+    scatter_start(1)
+    u0_scaled = alpha0 * u0[...]
+    l0[...] = u0_scaled
+    second = pltpu.make_async_copy(l0, sol_ref, out_sem.at[1])
+    second.start()
+    swap(1)
     import_margins(4)
     big_product(amat, al1)
-    gather_wait(1, 2)
-    solve(1)
-    scatter_start(1)
-    swap(1)
     mapped_in(1)
     apply_coarse(al1, al1)
     w0[...] = w0[...] - alpha0 * al1[...]
     dots = totals_start(1, rv, w0)
-    totals_spread(1, dots)
+    third = pltpu.make_async_copy(w0, image_ref, out_sem.at[2])
+    third.start()
     add_coarse(l1, l1)
     l1[...] = u0[...] - alpha0 * l1[...]
-    alpha1 = totals_finish(1)
-    sol_ref[...] = alpha0 * u0[...] + alpha1 * l1[...]
-    res_ref[...] = rv[...] - alpha1 * w0[...]
+    fourth = pltpu.make_async_copy(l1, update_ref, out_sem.at[3])
+    totals_spread(1, dots)
+    fourth.start()
+    alpha_ref[...] = totals_finish(1)
 
     for copy in pending:
         copy.wait_send()
     scatter_drain(0)
     scatter_drain(1)
+    for copy in (first, second, third, fourth):
+        copy.wait()
 
 
 def run(rhs, diagonal, couple, links, exports, linv, basis, cinv, owner):
@@ -602,9 +672,9 @@
         vm(field, F32),
         vm((K, OWN), F32),
         vm((1, OWN), F32),
-        vm((6, OWN), F32),
-        vm((6, OWN), jnp.int32),
-        vm((6, OVR), jnp.int32),
+        vm((6, 1, OWN), F32),
+        vm((6, 1, OWN), jnp.int32),
+        vm((6, 1, OVR), jnp.int32),
         vm((1, 128), jnp.int32),
         vm((LSLOTS, LCH, NEXT), F32),
         vm((2, OWN, NEXT), BF16),
@@ -620,8 +690,10 @@
         vm((2, 128, OWN), BF16),
         vm((2, OWN, K), BF16),
         vm((128, OWN), BF16),
-        vm((5, 6, OVR, NRHS), F32),
-        vm((5, 6, OVR, NRHS), F32),
+        vm((4, 6, OVR, NRHS), F32),
+        vm((4, 6, OVR, NRHS), F32),
+        vm((6, 128, 128), F32),
+        vm((6, 128, 128), F32),
         vm(field, F32),
         vm(field, F32),
         vm(field, F32),
@@ -646,20 +718,21 @@
         vm((2, 128, NRHS), F32),
         dma((8,)),
         dma((LSLOTS,)),
-        dma((2, 3, 3, 3)),
-        dma((2, 3, 3, 3)),
+        dma((2, 3, 6, 3)),
+        dma((2, 3, 6, 3)),
         dma((5, 6)),
         dma((5, 6)),
         dma((2,)),
         dma((2, 6)),
         dma((2, 4)),
+        dma((4,)),
     ]
     anywhere = pl.BlockSpec(memory_space=pl.ANY)
     return pl.pallas_call(
         kernel,
-        out_shape=(jax.ShapeDtypeStruct(field, F32), jax.ShapeDtypeStruct(field, F32)),
+        out_shape=[jax.ShapeDtypeStruct(field, F32)] * 4 + [jax.ShapeDtypeStruct((1, NRHS), F32)],
         in_specs=[anywhere] * 8 + [pl.BlockSpec(memory_space=pltpu.SMEM), anywhere],
-        out_specs=(pl.BlockSpec(memory_space=pltpu.VMEM), pl.BlockSpec(memory_space=pltpu.VMEM)),
+        out_specs=[anywhere] * 4 + [pl.BlockSpec(memory_space=pltpu.VMEM)],
         scratch_shapes=scratch,
         compiler_params=pltpu.CompilerParams(
             collective_id=0, has_side_effects=True, vmem_limit_bytes=63 * 1024 * 1024
@@ -669,18 +742,18 @@
 
 
 def body(rhs, diagonal, couple, neighbours, export_rows, local_inverse, basis, coarse_inverse, owner):
-    solution, residual = run(
+    first, update, residual, image, alpha = run(
         rhs.reshape(OWN, NRHS),
         diagonal.reshape(1, OWN),
-        couple.reshape(6, OWN),
-        neighbours.reshape(6, OWN),
-        export_rows.reshape(6, OVR),
+        couple.reshape(6, 1, OWN),
+        neighbours.reshape(6, 1, OWN),
+        export_rows.reshape(6, 1, OVR),
         local_inverse.reshape(OWN, NEXT),
         basis.reshape(K, OWN),
         coarse_inverse,
         owner,
     )
-    return solution.reshape(rhs.shape), residual.reshape(rhs.shape)
+    return (first + alpha * update).reshape(rhs.shape), (residual - alpha * image).reshape(rhs.shape)
 
 
 def solution(mesh):

time: 133 us -> 110 us (0.83)
  Pallas kernels: 124 us -> 107 us
  local copies, waits for them, and re-layouts: 7.74 us -> 0 us
  other arithmetic: 0 us -> 2.59 us
    pallas_call x1, Pallas kernels: 124 us -> 107 us  [run(): pl.pallas_call(kernel, out_shape=[jax.ShapeDtypeStruct(field, F32)] * 4 +...]
    unnamed x5 -> x0, local copies, waits for them, and re-layouts: 7.74 us -> none
    reshape x0 -> x1, other arithmetic: none -> 2.59 us  [body(): (residual - alpha * image).reshape(rhs.shape)]
where the time goes in v2:
time: 110 us
  Pallas kernels  107 us (97%)
  other arithmetic  2.59 us (2%)
    pallas_call x1, Pallas kernels, run(): pl.pallas_call(kernel, out_shape=[jax.ShapeDtypeStruct(field, F32)] * 4 +...  107 us
    reshape x1, other arithmetic, body(): (residual - alpha * image).reshape(rhs.shape)  2.59 us

profile of v2, /device:TPU:1, one launch (start us, length us, event | category | flops | bytes accessed | tf_op | source)
XLA Modules:
  0.0 110.2 jit_solution(5041766779740706177)
XLA Ops:
  0.6 107.0 %shard_map.104 = (f32[1024,128]{1,0:T(8,128)}, f32[1024,128]{1,0:T(8,128)}, f32[1024,128]{1,0:T(8,128)}, f32[1024,128]{1,0:T(8,128)}, f32[1,128]{1,0:T(1,128)}) custom-call(f32[1024,128]{1,0:T(8,128)} %bitcast.15, f32[1,1024]{1,0:T(1,128)} %bitcast.20, f32[6,1,1024]{2,1,0:T(1,128)} %bitcast.17, s32[6,1,1024]{2,1,0:T(1,128)} %bitcast.18, ...), custom_call_target="tpu_custom_call" | custom-call | flops 12000000000 | bytes 15000000 | tf_op jit(solution)/shard_map/pallas_call | solution.py:731
  107.6 2.6 %subtract_bitcast_fusion = (f32[1,1,1,1024,128]{4,3,2,1,0:T(8,128)}, f32[1,1,1,1024,128]{4,3,2,1,0:T(8,128)}) fusion(f32[1024,128]{1,0:T(8,128)} %get-tuple-element.10, f32[1024,128]{1,0:T(8,128)} %get-tuple-element.11, f32[128]{0:T(128)} %bitcast.13, f32[1024,128]{1,0:T(8,128)} %get-tuple-element.7, f32[1024,128]{1,0:T(8,128)} %get-tuple-element.9), kind=kLoop, calls=%fused_computation | loop fusion | flops 524288 | bytes 3146240 | tf_op jit(solution)/shard_map/reshape | solution.py:756

commit v3 on v2

--- a/solution.py
+++ b/solution.py
@@ -20,6 +20,9 @@
 LSLOTS = 4
 
 SHARES = ((0, 24, (2, 1, 0)), (24, 24, (0, 2, 1)), (48, 16, (1, 0, 2)))
+
+
+A1, A2, A3, A4 = 0, 0, 6, 10
 
 
 def split(x):
@@ -103,7 +106,6 @@
     bsend,
     brecv,
     l0,
-    al0,
     u0,
     w0,
     l1,
@@ -114,6 +116,10 @@
     mhl,
     tcol,
     ncol,
+    wrow,
+    trow,
+    bamat,
+    rmat,
     ecol,
     psrc,
     rbuf,
@@ -271,12 +277,11 @@
     def outgoing(n):
         out = margins(n)[0]
 
-        def step(d, carry):
-            p = dot(emat[pl.ds(pl.multiple_of(d * OVR, OVR), OVR), :], xhl[0:OWN, :])
-            out[d] = p[:, 0:NRHS] + p[:, NRHS:]
-            return carry
-
-        lax.fori_loop(0, 6, step, 0)
+        for d in range(0, 6, 2):
+            p = dot(emat[d * OVR : (d + 2) * OVR, :], xhl[0:OWN, :])
+            q = p[:, 0:NRHS] + p[:, NRHS:]
+            out[d] = q[0:OVR]
+            out[d + 1] = q[OVR:]
 
     def import_margins(n):
         margins_wait(n)
@@ -284,12 +289,22 @@
         for b in range(6):
             put_pair(xhl, OWN + b * OVR, into[b] * valid[b])
 
-    def big_product(mat, dst):
+    def product_owned(mat, dst):
         def step(i, carry):
             r = pl.multiple_of(i * 512, 512)
-            p = dot(mat[0, pl.ds(r, 512), :], xhl[...])
-            q = dot(mat[1, pl.ds(r, 512), :], xhl[:, 0:NRHS])
+            p = dot(mat[0, pl.ds(r, 512), 0:OWN], xhl[0:OWN, :])
+            q = dot(mat[1, pl.ds(r, 512), 0:OWN], xhl[0:OWN, 0:NRHS])
             dst[pl.ds(r, 512), :] = fold(p, q)
+            return carry
+
+        lax.fori_loop(0, OWN // 512, step, 0)
+
+    def product_margins(mat, dst):
+        def step(i, carry):
+            r = pl.multiple_of(i * 512, 512)
+            p = dot(mat[0, pl.ds(r, 512), OWN:], xhl[OWN:, :])
+            q = dot(mat[1, pl.ds(r, 512), OWN:], xhl[OWN:, 0:NRHS])
+            dst[pl.ds(r, 512), :] = dst[pl.ds(r, 512), :] + fold(p, q)
             return carry
 
         lax.fori_loop(0, OWN // 512, step, 0)
@@ -407,18 +422,17 @@
         tcol[d : d + 1, 0:OVR] = exports_v[d].astype(F32)
     ecol[...] = tcol[...][:, 0:OVR].T
 
-    def export_rows(d, carry):
-        def group(g, inner):
-            rows = ecol[pl.ds(pl.multiple_of(g * 32, 32), 32), :]
-            lane = lax.broadcasted_iota(jnp.int32, (32, 8), 1)
-            col = jnp.sum(jnp.where(lane == d, rows, 0.0), axis=1, keepdims=True).astype(jnp.int32)
-            cells = lax.broadcasted_iota(jnp.int32, (32, OWN), 1)
-            emat[pl.ds(pl.multiple_of(d * OVR + g * 32, 32), 32), :] = jnp.where(cells == col, 1.0, 0.0).astype(BF16)
-            return inner
-
-        return lax.fori_loop(0, OVR // 32, group, carry)
-
-    lax.fori_loop(0, 6, export_rows, 0)
+    def export_rows(g, carry):
+        r = pl.multiple_of(g * 16, 16)
+        rows = ecol[pl.ds(r, 16), :]
+        lanes = lax.broadcasted_iota(jnp.int32, (16, 128), 1)
+        one, zero = jnp.ones((16, 128), BF16), jnp.zeros((16, 128), BF16)
+        for d in range(6):
+            place_d = jnp.broadcast_to(rows[:, d : d + 1], (16, 128)).astype(jnp.int32).astype(jnp.int16)
+            for j in range(OWN // 128):
+                hit = (lanes + j * 128).astype(jnp.int16) == place_d
+                emat[pl.ds(d * OVR + r, 16), j * 128 : (j + 1) * 128] = jnp.where(hit, one, zero)
+        return carry
 
     pltpu.make_async_copy(cinv_v, cinv_v, in_sem.at[7]).wait()
     lane = lax.broadcasted_iota(jnp.int32, (K, 128), 1)
@@ -435,17 +449,21 @@
     def column_pair(m, kk):
         return jnp.where(lane < 64, column_block(2 * m, kk, 0), column_block(2 * m + 1, kk, 1))
 
-    def order_other(m, carry):
-        csend[:, pl.ds(pl.multiple_of(m * 128, 128), 128)] = column_pair(m, 1 - core)
+    def order_other(i, carry):
+        for m in range(4):
+            m = 4 * i + m
+            csend[:, pl.ds(pl.multiple_of(m * 128, 128), 128)] = column_pair(m, 1 - core)
         return carry
 
-    def order_mine(m, carry):
-        hi, lo = split(column_pair(m, core))
-        chl[0:64, pl.ds(pl.multiple_of(m * 128, 128), 128)] = hi
-        chl[128:192, pl.ds(pl.multiple_of(m * 128, 128), 128)] = lo
+    def order_mine(i, carry):
+        for m in range(4):
+            m = 4 * i + m
+            hi, lo = split(column_pair(m, core))
+            chl[0:64, pl.ds(pl.multiple_of(m * 128, 128), 128)] = hi
+            chl[128:192, pl.ds(pl.multiple_of(m * 128, 128), 128)] = lo
         return carry
 
-    lax.fori_loop(0, 32, order_other, 0)
+    lax.fori_loop(0, 8, order_other, 0)
 
     for i in (3, 4, 5):
         loads[i].wait()
@@ -466,41 +484,63 @@
         ncol[k : k + 1, :] = jnp.where(gone, -1, targets[k]).astype(F32)
     tcol[6:7, :] = centre
     ncol[6:7, :] = own_row.astype(F32)
-    al0[:, 0:8] = tcol[...].T
-    al0[:, 8:16] = ncol[...].T
-
-    def operator_rows(g, carry):
-        r = pl.multiple_of(g * 16, 16)
-        cols = al0[pl.ds(r, 16), 0:16]
-        values = [split(jnp.broadcast_to(cols[:, k : k + 1], (16, 128))) for k in range(7)]
-        places = [
-            jnp.broadcast_to(cols[:, 8 + k : 9 + k], (16, 128)).astype(jnp.int32).astype(jnp.int16) for k in range(7)
-        ]
+    tcol[7:8, :] = jnp.zeros((1, OWN), F32)
+    ncol[7:8, :] = jnp.full((1, OWN), -1.0, F32)
+
+    def by_groups(ref, into):
+        row = lax.broadcasted_iota(jnp.int32, (8, 128), 0)
+        part = lax.broadcasted_iota(jnp.int32, (8, 128), 1) // 16
+        for c in range(8):
+            block = ref[:, c * 128 : (c + 1) * 128]
+            turned = jnp.zeros((8, 128), F32)
+            for d in range(8):
+                moved = block if d == 0 else pltpu.roll(pltpu.roll(block, 8 - d, 0), 16 * d, 1)
+                turned = jnp.where((part - row + 8) % 8 == d, moved, turned)
+            into[c * 8 : (c + 1) * 8, :] = turned
+
+    by_groups(tcol, wrow)
+    by_groups(ncol, trow)
+
+    def operator_rows(i, carry):
         lanes = lax.broadcasted_iota(jnp.int32, (16, 128), 1)
-        for j in range(NEXT // 128):
-            cells = (lanes + j * 128).astype(jnp.int16)
-            hi = jnp.zeros((16, 128), BF16)
-            lo = jnp.zeros((16, 128), BF16)
-            for k in range(7 if j < OWN // 128 else 6):
-                hit = cells == places[k]
-                hi = jnp.where(hit, values[k][0], hi)
-                lo = jnp.where(hit, values[k][1], lo)
-            amat[0, pl.ds(r, 16), j * 128 : (j + 1) * 128] = hi
-            amat[1, pl.ds(r, 16), j * 128 : (j + 1) * 128] = lo
+        row = lax.broadcasted_iota(jnp.int32, (16, 128), 0)
+        cell = lanes % 16 == row
+        one, zero = jnp.ones((16, 128), BF16), jnp.zeros((16, 128), BF16)
+        for g in range(4):
+            g = 4 * i + g
+            w = jnp.broadcast_to(wrow[pl.ds(g, 1), :], (16, 128))
+            t = jnp.broadcast_to(trow[pl.ds(g, 1), :], (16, 128)).astype(jnp.int32)
+            high = lax.shift_right_arithmetic(t, 8)
+            low = (t - high * 256).astype(F32).astype(BF16)
+            whi, wlo = split(jnp.where(cell, w, 0.0))
+            tile = jnp.where(cell, high, -1).astype(F32).astype(BF16)
+            his, los = [], []
+            for j in range(NEXT // 256):
+                hit = tile == jnp.asarray(j, BF16)
+                his.append(jnp.where(hit, whi, zero))
+                los.append(jnp.where(hit, wlo, zero))
+            spots = [jnp.where((row + 16 * q).astype(F32).astype(BF16) == low, one, zero) for q in range(16)]
+            placed = dot_nt(jnp.concatenate(his + los, axis=0), jnp.concatenate(spots, axis=0)).astype(BF16)
+            r = pl.multiple_of(g * 16, 16)
+            for j in range(NEXT // 256):
+                amat[0, pl.ds(r, 16), j * 256 : (j + 1) * 256] = placed[16 * j : 16 * j + 16]
+                amat[1, pl.ds(r, 16), j * 256 : (j + 1) * 256] = placed[160 + 16 * j : 176 + 16 * j]
         return carry
 
     def build_operator(first, last):
         lax.fori_loop(first, last, operator_rows, 0)
 
+    build_operator(0, A1)
     pl.semaphore_wait(bar, len(near))
     gather_one(0)
     ccopy = send(csend, crecv, c_sem.at[0], c_sem.at[1], sister)
+    lax.fori_loop(0, OVR // 16, export_rows, 0)
     outgoing(0)
     margins_start(0)
-    build_operator(0, 6)
+    build_operator(A1, A2)
     gather_two(0)
-    lax.fori_loop(0, 32, order_mine, 0)
-    build_operator(6, 18)
+    lax.fori_loop(0, 8, order_mine, 0)
+    build_operator(A2, A3)
     gather_three(0)
 
     for c in range(NLCH):
@@ -517,41 +557,41 @@
         if c + LSLOTS < NLCH:
             load_chunk(c + LSLOTS).start()
 
+    product_owned(linv, l0)
     import_margins(0)
-    big_product(linv, l0)
+    product_margins(linv, l0)
     put_pair(xhl, 0, l0[...])
     outgoing(2)
-    build_operator(18, 40)
-
-    bcat[0, 0:K, :] = bhl[0:K, :]
-    bcat[0, K : 2 * K, :] = bhl[0:K, :]
-    bcat[1, 0:K, :] = bhl[K : 2 * K, :]
-    bcat[1, K : 2 * K, :] = bhl[K : 2 * K, :]
+    build_operator(A3, A4)
+
+    basis_t = basis_v[...].T
+    hi, lo = split(basis_t)
+    bt[0] = hi
+    bt[1] = lo
+    bcat[...] = jnp.concatenate([hi, hi, lo, lo], axis=1)
     lane_h = lax.broadcasted_iota(jnp.int32, (128, 128), 1)
-
-    def export_basis(d, carry):
-        rows = emat[pl.ds(pl.multiple_of(d * OVR, OVR), OVR), :]
-        p = dot_nt(rows, bcat[0]) + dot_nt(rows, bcat[1])
-        bsend[d] = jnp.where(lane_h < 64, p[0:128], p[128:256])
-        return carry
-
-    lax.fori_loop(0, 6, export_basis, 0)
+    for d in range(0, 6, 2):
+        p = dot(emat[d * OVR : (d + 2) * OVR, :], bcat[...])
+        q = p[:, 0:NRHS] + p[:, NRHS:]
+        bsend[d] = jnp.where(lane_h < 64, q[0:128], q[128:256])
+        bsend[d + 1] = jnp.where(lane_h < 64, q[256:384], q[384:512])
+
     ccopy.wait_recv()
 
     def sister_rows(m, carry):
-        cols = pl.ds(pl.multiple_of(m * 128, 128), 128)
+        cols = pl.ds(pl.multiple_of(m * 512, 512), 512)
         hi, lo = split(crecv[:, cols])
         chl[64:128, cols] = hi
         chl[192:256, cols] = lo
         return carry
 
-    lax.fori_loop(0, 32, sister_rows, 0)
+    lax.fori_loop(0, 8, sister_rows, 0)
     gather_done(0)
     margins_start(2)
     margins_start(1)
     solve(0)
     scatter_start(0)
-    build_operator(40, 64)
+    build_operator(A4, 16)
 
     loads[6].wait()
     r_ = lax.broadcasted_iota(jnp.int32, (512, 128), 0)
@@ -570,79 +610,86 @@
     block = (((ch_ // 16) * 2 + kk_) * 4 + (ch_ // 4) % 4) * 4 + ch_ % 4
     held = jnp.where(owner_v[...] == block, 1.0, 0.0).astype(BF16)
     sel[...] = dot_nt(wanted, held).astype(BF16)
+    for j in range(0, NEXT, 512):
+        p = dot(bhl[...], amat[0, :, j : j + 512])
+        hi, lo = split(p[0:K] + p[K:] + dot(bhl[0:K, :], amat[1, :, j : j + 512]))
+        bamat[0:K, j : j + 512] = hi
+        bamat[K:, j : j + 512] = lo
     swap(0)
 
-    import_margins(2)
-    big_product(amat, al0)
-    put_pair(xhl, 0, al0[...])
-    projected = stacked(bhl[...], xhl[0:OWN, :])
-
     margins_wait(1)
-    basis_t = basis_v[...].T
-    hi, lo = split(basis_t)
-    bt[0] = hi
-    bt[1] = lo
     hi, lo = split(jnp.concatenate([basis_t, jnp.zeros_like(basis_t)], axis=1))
-    xg[0:OWN, 0:128] = hi
-    xg[0:OWN, 128:256] = lo
+    rmat[0:OWN, 0:128] = hi
+    rmat[0:OWN, 128:256] = lo
     for b in range(6):
         mask = jnp.where((lane_h < 64) == (b % 2 == 0), valid[b], 0.0)
         top, bottom = brecv[b], pltpu.roll(brecv[b], 64, 1)
         if b % 2 == 1:
             top, bottom = bottom, top
-        put_pair(xg, OWN + b * OVR, top * mask)
-        put_pair(xg, OWN + b * OVR + 128, bottom * mask)
-
-    def coarse_columns(i, carry):
-        r = pl.multiple_of(i * 256, 256)
-        for j in range(4):
-            rows = slice(0, OWN) if j == 3 else slice(OWN + j * 512, OWN + (j + 1) * 512)
-            p = dot(amat[0, pl.ds(r, 256), rows], xg[rows, :])
-            q = dot(amat[1, pl.ds(r, 256), rows], xg[rows, 0:NRHS])
-            hi, lo = split(fold(p, q))
-            gmat[0, pl.ds(r, 256), j * 128 : (j + 1) * 128] = hi
-            gmat[1, pl.ds(r, 256), j * 128 : (j + 1) * 128] = lo
-        return carry
-
-    lax.fori_loop(0, OWN // 256, coarse_columns, 0)
-    p = dot(bhl[...], gmat[0])
-    h = p[0:K] + p[K:] + dot(bhl[0:K, :], gmat[1])
-    hi, lo = split(h)
-    hmat[0:K, :] = hi
-    hmat[K : 2 * K, :] = lo
-
+        put_pair(rmat, OWN + b * OVR, top * mask)
+        put_pair(rmat, OWN + b * OVR + 128, bottom * mask)
+    spans = [(OWN + j * 512, OWN + (j + 1) * 512) for j in range(3)] + [(0, OWN)]
+    for j, (start, stop) in enumerate(spans):
+        hi, lo = split(stacked(bamat[:, start:stop], rmat[start:stop, :]))
+        hmat[0:K, j * 128 : (j + 1) * 128] = hi
+        hmat[K:, j * 128 : (j + 1) * 128] = lo
+    import_margins(2)
+    projected = stacked(bamat[...], xhl[...])
     mapped_in(0)
 
     gat[1, x, y, z] = projected + stacked(hmat[...], mhl[...])
     gather_one(1)
-    apply_coarse(al0, w0)
+    add_coarse(l0, u0)
+    put_pair(xhl, 0, u0[...])
+    into = margins(2)[1]
+    for j in range(3):
+        start, stop = spans[j]
+        part = mhl[j * 128 : (j + 1) * 128, :]
+        more = fold(dot(rmat[start:stop, 0:NRHS], part), dot(rmat[start:stop, NRHS:], part[:, 0:NRHS]))
+        put_pair(xhl, start, into[2 * j] * valid[2 * j] + more[0:OVR])
+        put_pair(xhl, start + OVR, into[2 * j + 1] * valid[2 * j + 1] + more[OVR:])
+    product_owned(amat, w0)
+    product_margins(amat, w0)
     put_pair(xhl, 0, w0[...])
     outgoing(3)
     gather_two(1)
     margins_start(3)
     dots = totals_start(0, rv, w0)
-    add_coarse(l0, u0)
+    product_owned(linv, l1)
     gather_three(1)
     totals_spread(0, dots)
     import_margins(3)
-    big_product(linv, l1)
+    product_margins(linv, l1)
     put_pair(xhl, 0, l1[...])
     outgoing(4)
+    margins_start(4)
     alpha0 = totals_finish(0)
     rv[...] = rv[...] - alpha0 * w0[...]
     first = pltpu.make_async_copy(rv, res_ref, out_sem.at[0])
     first.start()
     gather_done(1)
-    margins_start(4)
     solve(1)
     scatter_start(1)
     u0_scaled = alpha0 * u0[...]
     l0[...] = u0_scaled
     second = pltpu.make_async_copy(l0, sol_ref, out_sem.at[1])
     second.start()
+    product_owned(amat, al1)
     swap(1)
     import_margins(4)
-    big_product(amat, al1)
+    product_margins(amat, al1)
+
+    def coarse_columns(i, carry):
+        r = pl.multiple_of(i * 512, 512)
+        for j, (start, stop) in enumerate(spans):
+            p = dot(amat[0, pl.ds(r, 512), start:stop], rmat[start:stop, :])
+            q = dot(amat[1, pl.ds(r, 512), start:stop], rmat[start:stop, 0:NRHS])
+            hi, lo = split(fold(p, q))
+            gmat[0, pl.ds(r, 512), j * 128 : (j + 1) * 128] = hi
+            gmat[1, pl.ds(r, 512), j * 128 : (j + 1) * 128] = lo
+        return carry
+
+    lax.fori_loop(0, OWN // 512, coarse_columns, 0)
     mapped_in(1)
     apply_coarse(al1, al1)
     w0[...] = w0[...] - alpha0 * al1[...]
@@ -687,7 +734,7 @@
         vm((2, 4, 4, 4, K, NRHS), F32),
         vm((4096, 256), BF16),
         vm((NEXT, 256), BF16),
-        vm((2, 128, OWN), BF16),
+        vm((OWN, 256), BF16),
         vm((2, OWN, K), BF16),
         vm((128, OWN), BF16),
         vm((4, 6, OVR, NRHS), F32),
@@ -699,13 +746,16 @@
         vm(field, F32),
         vm(field, F32),
         vm(field, F32),
-        vm(field, F32),
         vm((2, OWN, 512), BF16),
         vm((128, 512), BF16),
         vm((512, 128), BF16),
         vm((512, 256), BF16),
         vm((8, OWN), F32),
         vm((8, OWN), F32),
+        vm((64, 128), F32),
+        vm((64, 128), F32),
+        vm((128, NEXT), BF16),
+        vm((NEXT, 256), BF16),
         vm((OVR, 8), F32),
         vm((2, 2, CHIPS, NRHS), F32),
         vm((2, 2, CHIPS, NRHS), F32),

time: 110 us -> 100 us (0.909)
  Pallas kernels: 107 us -> 96.6 us
    pallas_call x1, Pallas kernels: 107 us -> 96.6 us  [run(): pl.pallas_call(kernel, out_shape=[jax.ShapeDtypeStruct(field, F32)] * 4 +...]
where the time goes in v3:
time: 100 us; the launch traced here: 99.8 us
  Pallas kernels  96.6 us (97%)
  other arithmetic  2.59 us (3%)
    pallas_call x1, Pallas kernels, run(): pl.pallas_call(kernel, out_shape=[jax.ShapeDtypeStruct(field, F32)] * 4 +...  96.6 us
    reshape x1, other arithmetic, body(): (residual - alpha * image).reshape(rhs.shape)  2.59 us

profile of v3, /device:TPU:1, one launch (start us, length us, event | category | flops | bytes accessed | tf_op | source)
XLA Modules:
  0.0 99.8 jit_solution(16472645311181646803)
XLA Ops:
  0.6 96.6 %shard_map.104 = (f32[1024,128]{1,0:T(8,128)}, f32[1024,128]{1,0:T(8,128)}, f32[1024,128]{1,0:T(8,128)}, f32[1024,128]{1,0:T(8,128)}, f32[1,128]{1,0:T(1,128)}) custom-call(f32[1024,128]{1,0:T(8,128)} %bitcast.15, f32[1,1024]{1,0:T(1,128)} %bitcast.20, f32[6,1,1024]{2,1,0:T(1,128)} %bitcast.17, s32[6,1,1024]{2,1,0:T(1,128)} %bitcast.18, ...), custom_call_target="tpu_custom_call" | custom-call | flops 12000000000 | bytes 15000000 | tf_op jit(solution)/shard_map/pallas_call | solution.py:781
  97.2 2.6 %subtract_bitcast_fusion = (f32[1,1,1,1024,128]{4,3,2,1,0:T(8,128)}, f32[1,1,1,1024,128]{4,3,2,1,0:T(8,128)}) fusion(f32[1024,128]{1,0:T(8,128)} %get-tuple-element.10, f32[1024,128]{1,0:T(8,128)} %get-tuple-element.11, f32[128]{0:T(128)} %bitcast.13, f32[1024,128]{1,0:T(8,128)} %get-tuple-element.7, f32[1024,128]{1,0:T(8,128)} %get-tuple-element.9), kind=kLoop, calls=%fused_computation | loop fusion | flops 524288 | bytes 3146240 | tf_op jit(solution)/shard_map/reshape | solution.py:806

commit v4 on v3

--- a/solution.py
+++ b/solution.py
@@ -19,10 +19,10 @@
 NLCH = OWN // LCH
 LSLOTS = 4
 
-SHARES = ((0, 24, (2, 1, 0)), (24, 24, (0, 2, 1)), (48, 16, (1, 0, 2)))
-
-
-A1, A2, A3, A4 = 0, 0, 6, 10
+SHARES = ((0, 22, (2, 1, 0)), (22, 21, (0, 2, 1)), (43, 21, (1, 0, 2)))
+
+
+A1, A2 = 2, 3
 
 
 def split(x):
@@ -370,13 +370,13 @@
 
     def apply_coarse(base, dst):
         def step(i, carry):
-            r = pl.multiple_of(i * 256, 256)
-            p = dot(gmat[0, pl.ds(r, 256), :], mhl[...])
-            q = dot(gmat[1, pl.ds(r, 256), :], mhl[:, 0:NRHS])
-            dst[pl.ds(r, 256), :] = base[pl.ds(r, 256), :] + fold(p, q)
+            r = pl.multiple_of(i * 512, 512)
+            p = dot(gmat[0, pl.ds(r, 512), :], mhl[...])
+            q = dot(gmat[1, pl.ds(r, 512), :], mhl[:, 0:NRHS])
+            dst[pl.ds(r, 512), :] = base[pl.ds(r, 512), :] + fold(p, q)
             return carry
 
-        lax.fori_loop(0, OWN // 256, step, 0)
+        lax.fori_loop(0, OWN // 512, step, 0)
 
     def totals_start(n, left, right):
         dsend[n] = jnp.zeros((8, NRHS), F32)
@@ -415,13 +415,6 @@
     bhl[K : 2 * K, :] = lo
     gat[0, x, y, z] = stacked(bhl[...], xhl[0:OWN, :])
 
-    loads[2].wait()
-    tcol[...] = jnp.zeros_like(tcol)
-    ncol[...] = jnp.zeros_like(ncol)
-    for d in range(6):
-        tcol[d : d + 1, 0:OVR] = exports_v[d].astype(F32)
-    ecol[...] = tcol[...][:, 0:OVR].T
-
     def export_rows(g, carry):
         r = pl.multiple_of(g * 16, 16)
         rows = ecol[pl.ds(r, 16), :]
@@ -464,6 +457,35 @@
         return carry
 
     lax.fori_loop(0, 8, order_other, 0)
+
+    def operator_rows(i, carry):
+        lanes = lax.broadcasted_iota(jnp.int32, (16, 128), 1)
+        row = lax.broadcasted_iota(jnp.int32, (16, 128), 0)
+        cell = lanes % 16 == row
+        one, zero = jnp.ones((16, 128), BF16), jnp.zeros((16, 128), BF16)
+        for g in range(8):
+            g = 8 * i + g
+            w = jnp.broadcast_to(wrow[pl.ds(g, 1), :], (16, 128))
+            t = jnp.broadcast_to(trow[pl.ds(g, 1), :], (16, 128)).astype(jnp.int32)
+            high = lax.shift_right_arithmetic(t, 8)
+            low = (t - high * 256).astype(F32).astype(BF16)
+            whi, wlo = split(jnp.where(cell, w, 0.0))
+            tile = jnp.where(cell, high, -1).astype(F32).astype(BF16)
+            his, los = [], []
+            for j in range(NEXT // 256):
+                hit = tile == jnp.asarray(j, BF16)
+                his.append(jnp.where(hit, whi, zero))
+                los.append(jnp.where(hit, wlo, zero))
+            spots = [jnp.where((row + 16 * q).astype(F32).astype(BF16) == low, one, zero) for q in range(16)]
+            placed = dot_nt(jnp.concatenate(his + los, axis=0), jnp.concatenate(spots, axis=0)).astype(BF16)
+            r = pl.multiple_of(g * 16, 16)
+            for j in range(NEXT // 256):
+                amat[0, pl.ds(r, 16), j * 256 : (j + 1) * 256] = placed[16 * j : 16 * j + 16]
+                amat[1, pl.ds(r, 16), j * 256 : (j + 1) * 256] = placed[160 + 16 * j : 176 + 16 * j]
+        return carry
+
+    def build_operator(first, last):
+        lax.fori_loop(first, last, operator_rows, 0)
 
     for i in (3, 4, 5):
         loads[i].wait()
@@ -501,49 +523,23 @@
     by_groups(tcol, wrow)
     by_groups(ncol, trow)
 
-    def operator_rows(i, carry):
-        lanes = lax.broadcasted_iota(jnp.int32, (16, 128), 1)
-        row = lax.broadcasted_iota(jnp.int32, (16, 128), 0)
-        cell = lanes % 16 == row
-        one, zero = jnp.ones((16, 128), BF16), jnp.zeros((16, 128), BF16)
-        for g in range(4):
-            g = 4 * i + g
-            w = jnp.broadcast_to(wrow[pl.ds(g, 1), :], (16, 128))
-            t = jnp.broadcast_to(trow[pl.ds(g, 1), :], (16, 128)).astype(jnp.int32)
-            high = lax.shift_right_arithmetic(t, 8)
-            low = (t - high * 256).astype(F32).astype(BF16)
-            whi, wlo = split(jnp.where(cell, w, 0.0))
-            tile = jnp.where(cell, high, -1).astype(F32).astype(BF16)
-            his, los = [], []
-            for j in range(NEXT // 256):
-                hit = tile == jnp.asarray(j, BF16)
-                his.append(jnp.where(hit, whi, zero))
-                los.append(jnp.where(hit, wlo, zero))
-            spots = [jnp.where((row + 16 * q).astype(F32).astype(BF16) == low, one, zero) for q in range(16)]
-            placed = dot_nt(jnp.concatenate(his + los, axis=0), jnp.concatenate(spots, axis=0)).astype(BF16)
-            r = pl.multiple_of(g * 16, 16)
-            for j in range(NEXT // 256):
-                amat[0, pl.ds(r, 16), j * 256 : (j + 1) * 256] = placed[16 * j : 16 * j + 16]
-                amat[1, pl.ds(r, 16), j * 256 : (j + 1) * 256] = placed[160 + 16 * j : 176 + 16 * j]
-        return carry
-
-    def build_operator(first, last):
-        lax.fori_loop(first, last, operator_rows, 0)
-
-    build_operator(0, A1)
     pl.semaphore_wait(bar, len(near))
     gather_one(0)
     ccopy = send(csend, crecv, c_sem.at[0], c_sem.at[1], sister)
+    loads[2].wait()
+    tcol[...] = jnp.zeros_like(tcol)
+    ncol[...] = jnp.zeros_like(ncol)
+    for d in range(6):
+        tcol[d : d + 1, 0:OVR] = exports_v[d].astype(F32)
+    ecol[...] = tcol[...][:, 0:OVR].T
+
     lax.fori_loop(0, OVR // 16, export_rows, 0)
     outgoing(0)
     margins_start(0)
-    build_operator(A1, A2)
     gather_two(0)
     lax.fori_loop(0, 8, order_mine, 0)
-    build_operator(A2, A3)
-    gather_three(0)
-
-    for c in range(NLCH):
+
+    def split_chunk(c):
         load_chunk(c).wait()
 
         def halves(g, carry):
@@ -557,12 +553,17 @@
         if c + LSLOTS < NLCH:
             load_chunk(c + LSLOTS).start()
 
+    for c in range(LSLOTS):
+        split_chunk(c)
+    gather_three(0)
+    for c in range(LSLOTS, NLCH):
+        split_chunk(c)
     product_owned(linv, l0)
+    build_operator(0, A1)
     import_margins(0)
     product_margins(linv, l0)
     put_pair(xhl, 0, l0[...])
     outgoing(2)
-    build_operator(A3, A4)
 
     basis_t = basis_v[...].T
     hi, lo = split(basis_t)
@@ -586,12 +587,13 @@
         return carry
 
     lax.fori_loop(0, 8, sister_rows, 0)
+    build_operator(A1, A2)
     gather_done(0)
     margins_start(2)
     margins_start(1)
     solve(0)
     scatter_start(0)
-    build_operator(A4, 16)
+    build_operator(A2, 8)
 
     loads[6].wait()
     r_ = lax.broadcasted_iota(jnp.int32, (512, 128), 0)
@@ -610,12 +612,13 @@
     block = (((ch_ // 16) * 2 + kk_) * 4 + (ch_ // 4) % 4) * 4 + ch_ % 4
     held = jnp.where(owner_v[...] == block, 1.0, 0.0).astype(BF16)
     sel[...] = dot_nt(wanted, held).astype(BF16)
+    swap(0)
+
     for j in range(0, NEXT, 512):
         p = dot(bhl[...], amat[0, :, j : j + 512])
         hi, lo = split(p[0:K] + p[K:] + dot(bhl[0:K, :], amat[1, :, j : j + 512]))
         bamat[0:K, j : j + 512] = hi
         bamat[K:, j : j + 512] = lo
-    swap(0)
 
     margins_wait(1)
     hi, lo = split(jnp.concatenate([basis_t, jnp.zeros_like(basis_t)], axis=1))
@@ -649,35 +652,14 @@
         put_pair(xhl, start, into[2 * j] * valid[2 * j] + more[0:OVR])
         put_pair(xhl, start + OVR, into[2 * j + 1] * valid[2 * j + 1] + more[OVR:])
     product_owned(amat, w0)
+    gather_two(1)
     product_margins(amat, w0)
     put_pair(xhl, 0, w0[...])
     outgoing(3)
-    gather_two(1)
+    gather_three(1)
     margins_start(3)
     dots = totals_start(0, rv, w0)
     product_owned(linv, l1)
-    gather_three(1)
-    totals_spread(0, dots)
-    import_margins(3)
-    product_margins(linv, l1)
-    put_pair(xhl, 0, l1[...])
-    outgoing(4)
-    margins_start(4)
-    alpha0 = totals_finish(0)
-    rv[...] = rv[...] - alpha0 * w0[...]
-    first = pltpu.make_async_copy(rv, res_ref, out_sem.at[0])
-    first.start()
-    gather_done(1)
-    solve(1)
-    scatter_start(1)
-    u0_scaled = alpha0 * u0[...]
-    l0[...] = u0_scaled
-    second = pltpu.make_async_copy(l0, sol_ref, out_sem.at[1])
-    second.start()
-    product_owned(amat, al1)
-    swap(1)
-    import_margins(4)
-    product_margins(amat, al1)
 
     def coarse_columns(i, carry):
         r = pl.multiple_of(i * 512, 512)
@@ -690,6 +672,26 @@
         return carry
 
     lax.fori_loop(0, OWN // 512, coarse_columns, 0)
+    totals_spread(0, dots)
+    gather_done(1)
+    solve(1)
+    scatter_start(1)
+    import_margins(3)
+    product_margins(linv, l1)
+    put_pair(xhl, 0, l1[...])
+    outgoing(4)
+    margins_start(4)
+    product_owned(amat, al1)
+    swap(1)
+    alpha0 = totals_finish(0)
+    rv[...] = rv[...] - alpha0 * w0[...]
+    first = pltpu.make_async_copy(rv, res_ref, out_sem.at[0])
+    first.start()
+    l0[...] = alpha0 * u0[...]
+    second = pltpu.make_async_copy(l0, sol_ref, out_sem.at[1])
+    second.start()
+    import_margins(4)
+    product_margins(amat, al1)
     mapped_in(1)
     apply_coarse(al1, al1)
     w0[...] = w0[...] - alpha0 * al1[...]

time: 100 us -> 91 us (0.910)
  Pallas kernels: 96.6 us -> 87.6 us
    pallas_call x1, Pallas kernels: 96.6 us -> 87.6 us  [run(): pl.pallas_call(kernel, out_shape=[jax.ShapeDtypeStruct(field, F32)] * 4 +...]
where the time goes in v4:
time: 91 us; the launch traced here: 90.9 us
  Pallas kernels  87.6 us (96%)
  other arithmetic  2.59 us (3%)
    pallas_call x1, Pallas kernels, run(): pl.pallas_call(kernel, out_shape=[jax.ShapeDtypeStruct(field, F32)] * 4 +...  87.6 us
    reshape x1, other arithmetic, body(): (residual - alpha * image).reshape(rhs.shape)  2.59 us

profile of v4, /device:TPU:1, one launch (start us, length us, event | category | flops | bytes accessed | tf_op | source)
XLA Modules:
  0.0 90.9 jit_solution(17438309984026699698)
XLA Ops:
  0.6 87.6 %shard_map.104 = (f32[1024,128]{1,0:T(8,128)}, f32[1024,128]{1,0:T(8,128)}, f32[1024,128]{1,0:T(8,128)}, f32[1024,128]{1,0:T(8,128)}, f32[1,128]{1,0:T(1,128)}) custom-call(f32[1024,128]{1,0:T(8,128)} %bitcast.15, f32[1,1024]{1,0:T(1,128)} %bitcast.20, f32[6,1,1024]{2,1,0:T(1,128)} %bitcast.17, s32[6,1,1024]{2,1,0:T(1,128)} %bitcast.18, ...), custom_call_target="tpu_custom_call" | custom-call | flops 12000000000 | bytes 15000000 | tf_op jit(solution)/shard_map/pallas_call | solution.py:783
  88.3 2.6 %subtract_bitcast_fusion = (f32[1,1,1,1024,128]{4,3,2,1,0:T(8,128)}, f32[1,1,1,1024,128]{4,3,2,1,0:T(8,128)}) fusion(f32[1024,128]{1,0:T(8,128)} %get-tuple-element.10, f32[1024,128]{1,0:T(8,128)} %get-tuple-element.11, f32[128]{0:T(128)} %bitcast.13, f32[1024,128]{1,0:T(8,128)} %get-tuple-element.7, f32[1024,128]{1,0:T(8,128)} %get-tuple-element.9), kind=kLoop, calls=%fused_computation | loop fusion | flops 524288 | bytes 3146240 | tf_op jit(solution)/shard_map/reshape | solution.py:808

commit v5 on v4

--- a/solution.py
+++ b/solution.py
@@ -535,8 +535,8 @@
 
     lax.fori_loop(0, OVR // 16, export_rows, 0)
     outgoing(0)
+    gather_two(0)
     margins_start(0)
-    gather_two(0)
     lax.fori_loop(0, 8, order_mine, 0)
 
     def split_chunk(c):
@@ -589,10 +589,10 @@
     lax.fori_loop(0, 8, sister_rows, 0)
     build_operator(A1, A2)
     gather_done(0)
-    margins_start(2)
-    margins_start(1)
     solve(0)
     scatter_start(0)
+    margins_start(1)
+    margins_start(2)
     build_operator(A2, 8)
 
     loads[6].wait()

time: 91 us -> 89.6 us (0.985)
  Pallas kernels: 87.6 us -> 86.2 us
    pallas_call x1, Pallas kernels: 87.6 us -> 86.2 us  [run(): pl.pallas_call(kernel, out_shape=[jax.ShapeDtypeStruct(field, F32)] * 4 +...]
where the time goes in v5:
time: 89.6 us; the launch traced here: 89.4 us
  Pallas kernels  86.2 us (96%)
  other arithmetic  2.59 us (3%)
    pallas_call x1, Pallas kernels, run(): pl.pallas_call(kernel, out_shape=[jax.ShapeDtypeStruct(field, F32)] * 4 +...  86.2 us
    reshape x1, other arithmetic, body(): (residual - alpha * image).reshape(rhs.shape)  2.59 us

profile of v5, /device:TPU:1, one launch (start us, length us, event | category | flops | bytes accessed | tf_op | source)
XLA Modules:
  0.0 89.4 jit_solution(10455781123339277985)
XLA Ops:
  0.6 86.2 %shard_map.104 = (f32[1024,128]{1,0:T(8,128)}, f32[1024,128]{1,0:T(8,128)}, f32[1024,128]{1,0:T(8,128)}, f32[1024,128]{1,0:T(8,128)}, f32[1,128]{1,0:T(1,128)}) custom-call(f32[1024,128]{1,0:T(8,128)} %bitcast.15, f32[1,1024]{1,0:T(1,128)} %bitcast.20, f32[6,1,1024]{2,1,0:T(1,128)} %bitcast.17, s32[6,1,1024]{2,1,0:T(1,128)} %bitcast.18, ...), custom_call_target="tpu_custom_call" | custom-call | flops 12000000000 | bytes 15000000 | tf_op jit(solution)/shard_map/pallas_call | solution.py:783
  86.8 2.6 %subtract_bitcast_fusion = (f32[1,1,1,1024,128]{4,3,2,1,0:T(8,128)}, f32[1,1,1,1024,128]{4,3,2,1,0:T(8,128)}) fusion(f32[1024,128]{1,0:T(8,128)} %get-tuple-element.10, f32[1024,128]{1,0:T(8,128)} %get-tuple-element.11, f32[128]{0:T(128)} %bitcast.13, f32[1024,128]{1,0:T(8,128)} %get-tuple-element.7, f32[1024,128]{1,0:T(8,128)} %get-tuple-element.9), kind=kLoop, calls=%fused_computation | loop fusion | flops 524288 | bytes 3146240 | tf_op jit(solution)/shard_map/reshape | solution.py:808
